TPU v7x, 256 devices: a whole 4x4x8 slice. The times are simulated.
256 devices in a mesh: gx: 16 (over z_hi, x), gy: 16 (over y, z_lo, core).
Axes of the slice: x: 4, y: 4, z: 8 (z_hi: 4, z_lo: 2; z = z_hi * 2 + z_lo), core: 2. Of those that a mesh axis runs over, the one named last changes fastest.
Arguments:
- noise: bfloat16 [1024, 1024, 128], P('gy', 'gx'), may hold values from -6 to 6
- cheb_coeff: float32 [6], replicated, may hold values from 0.4 to 1.2
- diag_x: float32 [1024, 64], P('gx'), may hold values from -0.165 to 0.165
- couple_x: bfloat16 [1024, 64], P('gx'), may hold values from -0.1640625 to 0.1640625
- diag_y: float32 [1024, 64], P('gy'), may hold values from -0.165 to 0.165
- couple_y: bfloat16 [1024, 64], P('gy'), may hold values from -0.1640625 to 0.1640625
- track_rows: int32 [128], P('gy'), may hold values from 0 to 1023, as said below
- track_obs: float32 [128, 1024], P('gy', 'gx'), may hold values from -6 to 6
- weights: float32 [1024, 128], P('gy'), may hold values from -0.5 to 0.5
Outputs:
- conditioned: float32 [1024, 1024, 128], P('gy', 'gx')
Inputs may be any that keep to these rules, and one draw needn't show every extreme that they name: `track_rows`: in block j of 8 entries (j from 0) the entries are distinct rows of j * 64 to j * 64 + 63; the block's first entry is its first row where j is even and its last row where j is odd.
All inputs are finite; a program needn't handle non-finite values.
Results may differ from a plain program's by a relative error of at most 0.0055.
Values may be sent and summed in bfloat16 or wider, within the bound.
No kernel may reach another device: no remote copies, remote signals or barrier semaphores. Data moves between devices by JAX's collectives and lax.ppermute only.
A program may use at most 64 MiB of HBM per device.

v0:
```python
import jax
import jax.numpy as jnp
from jax import lax
from jax.sharding import PartitionSpec as P

NUGGET = 0.3


def shifted(value, axis, steps):
    count = lax.axis_size(axis)
    leading, last = (max(0, -steps), min(count, count - steps))
    return lax.ppermute(value, axis, [(source, source + steps) for source in range(leading, last)])


def along_rows(matrix, field):
    return jnp.einsum("ij,yjs->yis", matrix, field, preferred_element_type=jnp.float32)


def along_rows_back(matrix, field):
    return jnp.einsum("ji,yjs->yis", matrix, field, preferred_element_type=jnp.float32)


def along_cols(matrix, field):
    flat = field.reshape(field.shape[0], -1)
    return jnp.dot(matrix, flat, preferred_element_type=jnp.float32).reshape(field.shape)


def along_cols_back(matrix, field):
    flat = field.reshape(field.shape[0], -1)
    return jnp.dot(matrix.T, flat, preferred_element_type=jnp.float32).reshape(field.shape)


def apply_rows(field, diag_x, couple_x, next_x):
    own = NUGGET * field + jnp.einsum(
        "ij,yjs->yis",
        diag_x,
        field,
        precision=lax.Precision.HIGHEST,
        preferred_element_type=jnp.float32,
    )
    rounded = field.astype(jnp.bfloat16)
    to_next = along_rows(next_x, rounded).astype(jnp.bfloat16)
    to_prev = along_rows_back(couple_x, rounded).astype(jnp.bfloat16)
    from_prev = shifted(to_next, "gx", 1)
    from_next = shifted(to_prev, "gx", -1)
    return own + from_prev.astype(jnp.float32) + from_next.astype(jnp.float32)


def apply_cols(field, diag_y, couple_y, next_y):
    height = field.shape[0]
    own = NUGGET * field + jnp.dot(
        diag_y,
        field.reshape(height, -1),
        precision=lax.Precision.HIGHEST,
        preferred_element_type=jnp.float32,
    ).reshape(field.shape)
    rounded = field.astype(jnp.bfloat16)
    to_next = along_cols(next_y, rounded).astype(jnp.bfloat16)
    to_prev = along_cols_back(couple_y, rounded).astype(jnp.bfloat16)
    from_prev = shifted(to_next, "gy", 1)
    from_next = shifted(to_prev, "gy", -1)
    return own + from_prev.astype(jnp.float32) + from_next.astype(jnp.float32)


def body(noise, cheb_coeff, diag_x, couple_x, diag_y, couple_y, track_rows, track_obs, weights):
    next_x = shifted(couple_x, "gx", -1)
    next_y = shifted(couple_y, "gy", -1)

    def operator(field):
        return apply_cols(apply_rows(field, diag_x, couple_x, next_x), diag_y, couple_y, next_y)

    start = noise.astype(jnp.float32)
    terms = cheb_coeff.shape[0]
    previous = start
    current = operator(start)
    total = cheb_coeff[0] * start
    total = total + cheb_coeff[1] * current
    for term in range(2, terms):
        following = 2.0 * operator(current) - previous
        previous = current
        current = following
        total = total + cheb_coeff[term] * current
    height = total.shape[0]
    first_row = lax.axis_index("gy") * height
    local_rows = track_rows - first_row
    picked = jnp.take(total, local_rows, axis=0)
    misfit = picked - track_obs[:, :, None]
    piece = lax.all_gather(misfit.astype(jnp.bfloat16), "gy", axis=0, tiled=True).astype(
        jnp.float32
    )
    flat = piece.reshape(piece.shape[0], -1)
    correction = jnp.dot(
        weights, flat, precision=lax.Precision.HIGHEST, preferred_element_type=jnp.float32
    )
    return total - correction.reshape(total.shape)


def solution(mesh):
    return jax.shard_map(
        body,
        mesh=mesh,
        in_specs=(
            P("gy", "gx", None),
            P(),
            P("gx", None),
            P("gx", None),
            P("gy", None),
            P("gy", None),
            P("gy"),
            P("gy", "gx"),
            P("gy", None),
        ),
        out_specs=P("gy", "gx", None),
        check_vma=False,
    )
```

profile of v0, /device:TPU:1, one launch (start us, length us, event | category | flops | bytes accessed | tf_op | source)
XLA Modules:
  0.0 516.0 jit_solution(14978060100930678665)
XLA Ops:
  16.7 5.1 collective-permute-start.3
  22.8 12.0 %collective-permute-done.2 = bf16[64,64,128]{2,1,0:T(8,128)(2,1)S(1)} collective-permute-done((bf16[64,64,128]{2,1,0:T(8,128)(2,1)S(1)}, bf16[64,64,128]{2,1,0:T(8,128)(2,1)S(1)}, u32[]{:S(2)}, u32[]{:S(2)}) %collective-permute-start.2) | collective-permute-done | bytes 1048608 | tf_op jit(solution)/shard_map/ppermute | solution.py:12
  39.0 7.5 %collective-permute-start.4 = (bf16[64,64,128]{2,1,0:T(8,128)(2,1)S(1)}, bf16[64,64,128]{2,1,0:T(8,128)(2,1)S(1)}, u32[]{:S(2)}, u32[]{:S(2)}) collective-permute-start(bf16[64,64,128]{2,1,0:T(8,128)(2,1)S(1)} %bitcast.313), channel_id=1, source_target_pairs={{0,1},{1,2},{2,3},{3,4},{4,5},{5,6},{6,7},{7,8},{8,9},{9,10},{10,1... | collective-permute-start | bytes 3145736 | tf_op jit(solution)/shard_map/ppermute | solution.py:12
  52.4 5.8 %collective-permute-done.4 = bf16[64,64,128]{2,1,0:T(8,128)(2,1)S(1)} collective-permute-done((bf16[64,64,128]{2,1,0:T(8,128)(2,1)S(1)}, bf16[64,64,128]{2,1,0:T(8,128)(2,1)S(1)}, u32[]{:S(2)}, u32[]{:S(2)}) %collective-permute-start.4) | collective-permute-done | bytes 1048608 | tf_op jit(solution)/shard_map/ppermute | solution.py:12
  58.3 28.2 %collective-permute-done.5 = bf16[64,64,128]{2,1,0:T(8,128)(2,1)S(1)} collective-permute-done((bf16[64,64,128]{2,1,0:T(8,128)(2,1)S(1)}, bf16[64,64,128]{2,1,0:T(8,128)(2,1)S(1)}, u32[]{:S(2)}, u32[]{:S(2)}) %collective-permute-start.5) | collective-permute-done | bytes 1048608 | tf_op jit(solution)/shard_map/ppermute | solution.py:12
  90.9 10.2 %collective-permute-done.6 = bf16[64,64,128]{2,1,0:T(8,128)(2,1)S(1)} collective-permute-done((bf16[64,64,128]{2,1,0:T(8,128)(2,1)S(1)}, bf16[64,64,128]{2,1,0:T(8,128)(2,1)S(1)}, u32[]{:S(2)}, u32[]{:S(2)}) %collective-permute-start.6) | collective-permute-done | bytes 1048608 | tf_op jit(solution)/shard_map/ppermute | solution.py:12
  109.6 13.2 %collective-permute-start.8 = (bf16[64,64,128]{2,1,0:T(8,128)(2,1)S(1)}, bf16[64,64,128]{2,1,0:T(8,128)(2,1)S(1)}, u32[]{:S(2)}, u32[]{:S(2)}) collective-permute-start(bf16[64,64,128]{2,1,0:T(8,128)(2,1)S(1)} %bitcast.314), channel_id=1, source_target_pairs={{0,1},{1,2},{2,3},{3,4},{4,5},{5,6},{6,7},{7,8},{8,9},{9,10},{10,1... | collective-permute-start | bytes 3145736 | tf_op jit(solution)/shard_map/ppermute | solution.py:12
  128.7 5.9 %collective-permute-done.8 = bf16[64,64,128]{2,1,0:T(8,128)(2,1)S(1)} collective-permute-done((bf16[64,64,128]{2,1,0:T(8,128)(2,1)S(1)}, bf16[64,64,128]{2,1,0:T(8,128)(2,1)S(1)}, u32[]{:S(2)}, u32[]{:S(2)}) %collective-permute-start.8) | collective-permute-done | bytes 1048608 | tf_op jit(solution)/shard_map/ppermute | solution.py:12
  134.5 26.2 %collective-permute-done.9 = bf16[64,64,128]{2,1,0:T(8,128)(2,1)S(1)} collective-permute-done((bf16[64,64,128]{2,1,0:T(8,128)(2,1)S(1)}, bf16[64,64,128]{2,1,0:T(8,128)(2,1)S(1)}, u32[]{:S(2)}, u32[]{:S(2)}) %collective-permute-start.9) | collective-permute-done | bytes 1048608 | tf_op jit(solution)/shard_map/ppermute | solution.py:12
  165.8 10.1 %collective-permute-done.10 = bf16[64,64,128]{2,1,0:T(8,128)(2,1)S(1)} collective-permute-done((bf16[64,64,128]{2,1,0:T(8,128)(2,1)S(1)}, bf16[64,64,128]{2,1,0:T(8,128)(2,1)S(1)}, u32[]{:S(2)}, u32[]{:S(2)}) %collective-permute-start.10) | collective-permute-done | bytes 1048608 | tf_op jit(solution)/shard_map/ppermute | solution.py:12
  175.9 7.5 %collective-permute-done.11 = bf16[64,64,128]{2,1,0:T(8,128)(2,1)S(1)} collective-permute-done((bf16[64,64,128]{2,1,0:T(8,128)(2,1)S(1)}, bf16[64,64,128]{2,1,0:T(8,128)(2,1)S(1)}, u32[]{:S(2)}, u32[]{:S(2)}) %collective-permute-start.11) | collective-permute-done | bytes 1048608 | tf_op jit(solution)/shard_map/ppermute | solution.py:12
  188.0 12.6 %collective-permute-start.12 = (bf16[64,64,128]{2,1,0:T(8,128)(2,1)S(1)}, bf16[64,64,128]{2,1,0:T(8,128)(2,1)S(1)}, u32[]{:S(2)}, u32[]{:S(2)}) collective-permute-start(bf16[64,64,128]{2,1,0:T(8,128)(2,1)S(1)} %bitcast.315), channel_id=1, source_target_pairs={{0,1},{1,2},{2,3},{3,4},{4,5},{5,6},{6,7},{7,8},{8,9},{9,10},{10,1... | collective-permute-start | bytes 3145736 | tf_op jit(solution)/shard_map/ppermute | solution.py:12
  206.6 5.9 %collective-permute-done.12 = bf16[64,64,128]{2,1,0:T(8,128)(2,1)S(1)} collective-permute-done((bf16[64,64,128]{2,1,0:T(8,128)(2,1)S(1)}, bf16[64,64,128]{2,1,0:T(8,128)(2,1)S(1)}, u32[]{:S(2)}, u32[]{:S(2)}) %collective-permute-start.12) | collective-permute-done | bytes 1048608 | tf_op jit(solution)/shard_map/ppermute | solution.py:12
  212.4 10.1 %collective-permute-done.13 = bf16[64,64,128]{2,1,0:T(8,128)(2,1)S(1)} collective-permute-done((bf16[64,64,128]{2,1,0:T(8,128)(2,1)S(1)}, bf16[64,64,128]{2,1,0:T(8,128)(2,1)S(1)}, u32[]{:S(2)}, u32[]{:S(2)}) %collective-permute-start.13) | collective-permute-done | bytes 1048608 | tf_op jit(solution)/shard_map/ppermute | solution.py:12
  224.4 16.6 %collective-permute-start.14 = (bf16[64,64,128]{2,1,0:T(8,128)(2,1)S(1)}, bf16[64,64,128]{2,1,0:T(8,128)(2,1)S(1)}, u32[]{:S(2)}, u32[]{:S(2)}) collective-permute-start(bf16[64,64,128]{2,1,0:T(8,128)(2,1)S(1)} %fusion.78), channel_id=1, source_target_pairs={{0,16},{16,32},{32,48},{48,64},{64,80},{80,96},{96,112},{112,128},... | collective-permute-start | bytes 3145736 | tf_op jit(solution)/shard_map/ppermute | solution.py:12
  242.8 10.0 %collective-permute-done.14 = bf16[64,64,128]{2,1,0:T(8,128)(2,1)S(1)} collective-permute-done((bf16[64,64,128]{2,1,0:T(8,128)(2,1)S(1)}, bf16[64,64,128]{2,1,0:T(8,128)(2,1)S(1)}, u32[]{:S(2)}, u32[]{:S(2)}) %collective-permute-start.14) | collective-permute-done | bytes 1048608 | tf_op jit(solution)/shard_map/ppermute | solution.py:12
  270.3 5.9 %collective-permute-done.16 = bf16[64,64,128]{2,1,0:T(8,128)(2,1)S(1)} collective-permute-done((bf16[64,64,128]{2,1,0:T(8,128)(2,1)S(1)}, bf16[64,64,128]{2,1,0:T(8,128)(2,1)S(1)}, u32[]{:S(2)}, u32[]{:S(2)}) %collective-permute-start.16) | collective-permute-done | bytes 1048608 | tf_op jit(solution)/shard_map/ppermute | solution.py:12
  276.2 33.4 %collective-permute-done.17 = bf16[64,64,128]{2,1,0:T(8,128)(2,1)S(1)} collective-permute-done((bf16[64,64,128]{2,1,0:T(8,128)(2,1)S(1)}, bf16[64,64,128]{2,1,0:T(8,128)(2,1)S(1)}, u32[]{:S(2)}, u32[]{:S(2)}) %collective-permute-start.17) | collective-permute-done | bytes 1048608 | tf_op jit(solution)/shard_map/ppermute | solution.py:12
  311.6 13.4 %collective-permute-start.18 = (bf16[64,64,128]{2,1,0:T(8,128)(2,1)S(1)}, bf16[64,64,128]{2,1,0:T(8,128)(2,1)S(1)}, u32[]{:S(2)}, u32[]{:S(2)}) collective-permute-start(bf16[64,64,128]{2,1,0:T(8,128)(2,1)S(1)} %fusion.79), channel_id=1, source_target_pairs={{0,16},{16,32},{32,48},{48,64},{64,80},{80,96},{96,112},{112,128},... | collective-permute-start | bytes 3145736 | tf_op jit(solution)/shard_map/ppermute | solution.py:12
  326.4 10.2 %collective-permute-done.18 = bf16[64,64,128]{2,1,0:T(8,128)(2,1)S(1)} collective-permute-done((bf16[64,64,128]{2,1,0:T(8,128)(2,1)S(1)}, bf16[64,64,128]{2,1,0:T(8,128)(2,1)S(1)}, u32[]{:S(2)}, u32[]{:S(2)}) %collective-permute-start.18) | collective-permute-done | bytes 1048608 | tf_op jit(solution)/shard_map/ppermute | solution.py:12
  354.8 4.9 fusion.64
  362.4 38.0 %collective-permute-done.21 = bf16[64,64,128]{2,1,0:T(8,128)(2,1)} collective-permute-done((bf16[64,64,128]{2,1,0:T(8,128)(2,1)}, bf16[64,64,128]{2,1,0:T(8,128)(2,1)}, u32[]{:S(2)}, u32[]{:S(2)}) %collective-permute-start.21) | collective-permute-done | bytes 1048608 | tf_op jit(solution)/shard_map/ppermute | solution.py:12
  400.4 8.6 %fusion.4 = f32[64,64,128]{2,1,0:T(8,128)} fusion(bf16[64,64,128]{2,1,0:T(8,128)(2,1)S(1)} %copy-done.7, f32[64,64,128]{2,1,0:T(8,128)S(1)} %copy-done.4, f32[8,8,64,128]{3,2,1,0:T(8,128)S(1)} %copy.51, bf16[64,64,128]{2,1,0:T(8,128)(2,1)} %collective-permute-done.21, bf16[64,64,128]{2,1,0:T(8,128)(2,1)} %collective-permute-done.20, ...), kind=kLoop, calls=%fused_computation.18 | loop fusion | flops 10485760 | bytes 17825816 | tf_op jit(solution)/shard_map/add | solution.py:82
  412.0 90.0 %all-gather.2.cloned.1.call-done = bf16[128,64,128]{2,1,0:T(8,128)(2,1)} async-done(((bf16[8,64,128]{2,1,0:T(8,128)(2,1)}), bf16[128,64,128]{2,1,0:T(8,128)(2,1)}) %all-gather.2.cloned.1.call-update) | async-done | bytes 2097168 | tf_op jit(solution)/shard_map/all_gather | solution.py:88
  (116 shorter events, 110.5 us)
Async XLA Ops:
  6.5 495.4 %all-gather.2.cloned.1.call-start = ((), (), s32[]{:S(2)}) async-start(), calls=%async_computation | async-start | bytes 2228224 | tf_op jit(solution)/shard_map/all_gather | solution.py:88
  6.5 5.4 %collective-permute-start = (bf16[64,64]{1,0:T(8,128)(2,1)}, bf16[64,64]{1,0:T(8,128)(2,1)S(1)}, u32[]{:S(2)}, u32[]{:S(2)}) collective-permute-start(bf16[64,64]{1,0:T(8,128)(2,1)} %param.12), channel_id=1, source_target_pairs={{16,0},{32,16},{48,32},{64,48},{80,64},{96,80},{112,96},{128,112},... | collective-permute-start | bytes 24584 | tf_op jit(solution)/shard_map/ppermute | solution.py:12
  9.7 25.1 %collective-permute-start.2 = (bf16[64,64,128]{2,1,0:T(8,128)(2,1)S(1)}, bf16[64,64,128]{2,1,0:T(8,128)(2,1)S(1)}, u32[]{:S(2)}, u32[]{:S(2)}) collective-permute-start(bf16[64,64,128]{2,1,0:T(8,128)(2,1)S(1)} %fusion.70), channel_id=1, source_target_pairs={{16,0},{32,16},{48,32},{64,48},{80,64},{96,80},{112,96},{128,112},... | collective-permute-start | bytes 3145736 | tf_op jit(solution)/shard_map/ppermute | solution.py:12
  12.4 23.8 %collective-permute-start.1 = (bf16[64,64,128]{2,1,0:T(8,128)(2,1)S(1)}, bf16[64,64,128]{2,1,0:T(8,128)(2,1)S(1)}, u32[]{:S(2)}, u32[]{:S(2)}) collective-permute-start(bf16[64,64,128]{2,1,0:T(8,128)(2,1)S(1)} %fusion.75), channel_id=1, source_target_pairs={{0,16},{16,32},{32,48},{48,64},{64,80},{80,96},{96,112},{112,128},... | collective-permute-start | bytes 3145736 | tf_op jit(solution)/shard_map/ppermute | solution.py:12
  16.7 21.1 %collective-permute-start.3 = (bf16[64,64]{1,0:T(8,128)(2,1)S(1)}, bf16[64,64]{1,0:T(8,128)(2,1)S(1)}, u32[]{:S(2)}, u32[]{:S(2)}) collective-permute-start(bf16[64,64]{1,0:T(8,128)(2,1)S(1)} %copy-done.12), channel_id=1, source_target_pairs={{1,0},{2,1},{3,2},{4,3},{5,4},{6,5},{7,6},{8,7},{9,8},{10,9},{11,1... | collective-permute-start | bytes 24584 | tf_op jit(solution)/shard_map/ppermute | solution.py:12
  39.0 19.3 %collective-permute-start.4 = (bf16[64,64,128]{2,1,0:T(8,128)(2,1)S(1)}, bf16[64,64,128]{2,1,0:T(8,128)(2,1)S(1)}, u32[]{:S(2)}, u32[]{:S(2)}) collective-permute-start(bf16[64,64,128]{2,1,0:T(8,128)(2,1)S(1)} %bitcast.313), channel_id=1, source_target_pairs={{0,1},{1,2},{2,3},{3,4},{4,5},{5,6},{6,7},{7,8},{8,9},{9,10},{10,1... | collective-permute-start | bytes 3145736 | tf_op jit(solution)/shard_map/ppermute | solution.py:12
  46.8 39.7 %collective-permute-start.5 = (bf16[64,64,128]{2,1,0:T(8,128)(2,1)S(1)}, bf16[64,64,128]{2,1,0:T(8,128)(2,1)S(1)}, u32[]{:S(2)}, u32[]{:S(2)}) collective-permute-start(bf16[64,64,128]{2,1,0:T(8,128)(2,1)S(1)} %bitcast.317), channel_id=1, source_target_pairs={{1,0},{2,1},{3,2},{4,3},{5,4},{6,5},{7,6},{8,7},{9,8},{10,9},{11,1... | collective-permute-start | bytes 3145736 | tf_op jit(solution)/shard_map/ppermute | solution.py:12
  88.1 13.0 %collective-permute-start.6 = (bf16[64,64,128]{2,1,0:T(8,128)(2,1)S(1)}, bf16[64,64,128]{2,1,0:T(8,128)(2,1)S(1)}, u32[]{:S(2)}, u32[]{:S(2)}) collective-permute-start(bf16[64,64,128]{2,1,0:T(8,128)(2,1)S(1)} %fusion.76), channel_id=1, source_target_pairs={{0,16},{16,32},{32,48},{48,64},{64,80},{80,96},{96,112},{112,128},... | collective-permute-start | bytes 3145736 | tf_op jit(solution)/shard_map/ppermute | solution.py:12
  89.4 15.5 %collective-permute-start.7 = (bf16[64,64,128]{2,1,0:T(8,128)(2,1)S(1)}, bf16[64,64,128]{2,1,0:T(8,128)(2,1)S(1)}, u32[]{:S(2)}, u32[]{:S(2)}) collective-permute-start(bf16[64,64,128]{2,1,0:T(8,128)(2,1)S(1)} %fusion.71), channel_id=1, source_target_pairs={{16,0},{32,16},{48,32},{64,48},{80,64},{96,80},{112,96},{128,112},... | collective-permute-start | bytes 3145736 | tf_op jit(solution)/shard_map/ppermute | solution.py:12
  109.6 24.9 %collective-permute-start.8 = (bf16[64,64,128]{2,1,0:T(8,128)(2,1)S(1)}, bf16[64,64,128]{2,1,0:T(8,128)(2,1)S(1)}, u32[]{:S(2)}, u32[]{:S(2)}) collective-permute-start(bf16[64,64,128]{2,1,0:T(8,128)(2,1)S(1)} %bitcast.314), channel_id=1, source_target_pairs={{0,1},{1,2},{2,3},{3,4},{4,5},{5,6},{6,7},{7,8},{8,9},{9,10},{10,1... | collective-permute-start | bytes 3145736 | tf_op jit(solution)/shard_map/ppermute | solution.py:12
  123.1 37.6 %collective-permute-start.9 = (bf16[64,64,128]{2,1,0:T(8,128)(2,1)S(1)}, bf16[64,64,128]{2,1,0:T(8,128)(2,1)S(1)}, u32[]{:S(2)}, u32[]{:S(2)}) collective-permute-start(bf16[64,64,128]{2,1,0:T(8,128)(2,1)S(1)} %bitcast.318), channel_id=1, source_target_pairs={{1,0},{2,1},{3,2},{4,3},{5,4},{6,5},{7,6},{8,7},{9,8},{10,9},{11,1... | collective-permute-start | bytes 3145736 | tf_op jit(solution)/shard_map/ppermute | solution.py:12
  161.6 147.9 %copy-start.1 = (f32[64,64,128]{2,1,0:T(8,128)}, f32[64,64,128]{2,1,0:T(8,128)S(1)}, u32[]{:S(2)}) copy-start(f32[64,64,128]{2,1,0:T(8,128)S(1)} %convert_subtract_fusion) | copy-start | bytes 6291460
  162.6 13.3 %collective-permute-start.10 = (bf16[64,64,128]{2,1,0:T(8,128)(2,1)S(1)}, bf16[64,64,128]{2,1,0:T(8,128)(2,1)S(1)}, u32[]{:S(2)}, u32[]{:S(2)}) collective-permute-start(bf16[64,64,128]{2,1,0:T(8,128)(2,1)S(1)} %fusion.77), channel_id=1, source_target_pairs={{0,16},{16,32},{32,48},{48,64},{64,80},{80,96},{96,112},{112,128},... | collective-permute-start | bytes 3145736 | tf_op jit(solution)/shard_map/ppermute | solution.py:12
  164.2 19.1 %collective-permute-start.11 = (bf16[64,64,128]{2,1,0:T(8,128)(2,1)S(1)}, bf16[64,64,128]{2,1,0:T(8,128)(2,1)S(1)}, u32[]{:S(2)}, u32[]{:S(2)}) collective-permute-start(bf16[64,64,128]{2,1,0:T(8,128)(2,1)S(1)} %fusion.72), channel_id=1, source_target_pairs={{16,0},{32,16},{48,32},{64,48},{80,64},{96,80},{112,96},{128,112},... | collective-permute-start | bytes 3145736 | tf_op jit(solution)/shard_map/ppermute | solution.py:12
  188.0 24.4 %collective-permute-start.12 = (bf16[64,64,128]{2,1,0:T(8,128)(2,1)S(1)}, bf16[64,64,128]{2,1,0:T(8,128)(2,1)S(1)}, u32[]{:S(2)}, u32[]{:S(2)}) collective-permute-start(bf16[64,64,128]{2,1,0:T(8,128)(2,1)S(1)} %bitcast.315), channel_id=1, source_target_pairs={{0,1},{1,2},{2,3},{3,4},{4,5},{5,6},{6,7},{7,8},{8,9},{9,10},{10,1... | collective-permute-start | bytes 3145736 | tf_op jit(solution)/shard_map/ppermute | solution.py:12
  201.0 21.6 %collective-permute-start.13 = (bf16[64,64,128]{2,1,0:T(8,128)(2,1)S(1)}, bf16[64,64,128]{2,1,0:T(8,128)(2,1)S(1)}, u32[]{:S(2)}, u32[]{:S(2)}) collective-permute-start(bf16[64,64,128]{2,1,0:T(8,128)(2,1)S(1)} %bitcast.319), channel_id=1, source_target_pairs={{1,0},{2,1},{3,2},{4,3},{5,4},{6,5},{7,6},{8,7},{9,8},{10,9},{11,1... | collective-permute-start | bytes 3145736 | tf_op jit(solution)/shard_map/ppermute | solution.py:12
  224.4 28.3 %collective-permute-start.14 = (bf16[64,64,128]{2,1,0:T(8,128)(2,1)S(1)}, bf16[64,64,128]{2,1,0:T(8,128)(2,1)S(1)}, u32[]{:S(2)}, u32[]{:S(2)}) collective-permute-start(bf16[64,64,128]{2,1,0:T(8,128)(2,1)S(1)} %fusion.78), channel_id=1, source_target_pairs={{0,16},{16,32},{32,48},{48,64},{64,80},{80,96},{96,112},{112,128},... | collective-permute-start | bytes 3145736 | tf_op jit(solution)/shard_map/ppermute | solution.py:12
  241.1 15.5 %collective-permute-start.15 = (bf16[64,64,128]{2,1,0:T(8,128)(2,1)S(1)}, bf16[64,64,128]{2,1,0:T(8,128)(2,1)S(1)}, u32[]{:S(2)}, u32[]{:S(2)}) collective-permute-start(bf16[64,64,128]{2,1,0:T(8,128)(2,1)S(1)} %fusion.73), channel_id=1, source_target_pairs={{16,0},{32,16},{48,32},{64,48},{80,64},{96,80},{112,96},{128,112},... | collective-permute-start | bytes 3145736 | tf_op jit(solution)/shard_map/ppermute | solution.py:12
  261.3 14.9 %collective-permute-start.16 = (bf16[64,64,128]{2,1,0:T(8,128)(2,1)S(1)}, bf16[64,64,128]{2,1,0:T(8,128)(2,1)S(1)}, u32[]{:S(2)}, u32[]{:S(2)}) collective-permute-start(bf16[64,64,128]{2,1,0:T(8,128)(2,1)S(1)} %bitcast.316), channel_id=1, source_target_pairs={{0,1},{1,2},{2,3},{3,4},{4,5},{5,6},{6,7},{7,8},{8,9},{9,10},{10,1... | collective-permute-start | bytes 3145736 | tf_op jit(solution)/shard_map/ppermute | solution.py:12
  264.7 44.8 %collective-permute-start.17 = (bf16[64,64,128]{2,1,0:T(8,128)(2,1)S(1)}, bf16[64,64,128]{2,1,0:T(8,128)(2,1)S(1)}, u32[]{:S(2)}, u32[]{:S(2)}) collective-permute-start(bf16[64,64,128]{2,1,0:T(8,128)(2,1)S(1)} %bitcast.320), channel_id=1, source_target_pairs={{1,0},{2,1},{3,2},{4,3},{5,4},{6,5},{7,6},{8,7},{9,8},{10,9},{11,1... | collective-permute-start | bytes 3145736 | tf_op jit(solution)/shard_map/ppermute | solution.py:12
  311.6 25.0 %collective-permute-start.18 = (bf16[64,64,128]{2,1,0:T(8,128)(2,1)S(1)}, bf16[64,64,128]{2,1,0:T(8,128)(2,1)S(1)}, u32[]{:S(2)}, u32[]{:S(2)}) collective-permute-start(bf16[64,64,128]{2,1,0:T(8,128)(2,1)S(1)} %fusion.79), channel_id=1, source_target_pairs={{0,16},{16,32},{32,48},{48,64},{64,80},{80,96},{96,112},{112,128},... | collective-permute-start | bytes 3145736 | tf_op jit(solution)/shard_map/ppermute | solution.py:12
  324.9 15.5 %collective-permute-start.19 = (bf16[64,64,128]{2,1,0:T(8,128)(2,1)S(1)}, bf16[64,64,128]{2,1,0:T(8,128)(2,1)S(1)}, u32[]{:S(2)}, u32[]{:S(2)}) collective-permute-start(bf16[64,64,128]{2,1,0:T(8,128)(2,1)S(1)} %fusion.74), channel_id=1, source_target_pairs={{16,0},{32,16},{48,32},{64,48},{80,64},{96,80},{112,96},{128,112},... | collective-permute-start | bytes 3145736 | tf_op jit(solution)/shard_map/ppermute | solution.py:12
  347.5 14.9 %collective-permute-start.20 = (bf16[64,64,128]{2,1,0:T(8,128)(2,1)}, bf16[64,64,128]{2,1,0:T(8,128)(2,1)}, u32[]{:S(2)}, u32[]{:S(2)}) collective-permute-start(bf16[64,64,128]{2,1,0:T(8,128)(2,1)} %bitcast.91), channel_id=1, source_target_pairs={{0,1},{1,2},{2,3},{3,4},{4,5},{5,6},{6,7},{7,8},{8,9},{9,10},{10,1... | collective-permute-start | bytes 3145736 | tf_op jit(solution)/shard_map/ppermute | solution.py:12
  351.6 48.7 %collective-permute-start.21 = (bf16[64,64,128]{2,1,0:T(8,128)(2,1)}, bf16[64,64,128]{2,1,0:T(8,128)(2,1)}, u32[]{:S(2)}, u32[]{:S(2)}) collective-permute-start(bf16[64,64,128]{2,1,0:T(8,128)(2,1)} %bitcast.93), channel_id=1, source_target_pairs={{1,0},{2,1},{3,2},{4,3},{5,4},{6,5},{7,6},{8,7},{9,8},{10,9},{11,1... | collective-permute-start | bytes 3145736 | tf_op jit(solution)/shard_map/ppermute | solution.py:12
  (16 other events, 440.8 us)
Sparse Core Ops, SparseCore 0:
  412.1 89.8 all-gather.1
where the time goes:
time: 525 us; the launch traced here: 516 us
  waiting for transfers between devices  326 us (62%)
  starting transfers between devices  101 us (19%)
  matrix products  48.8 us (9%)
  other arithmetic  15.5 us (3%)
  between operations  14.3 us (3%)
  local copies, waits for them, and re-layouts  11 us (2%)
    ppermute x22, waiting for transfers between devices, shifted(): lax.ppermute(value, axis, [(source, source + steps) for source in range(l...  236 us
    ppermute x22, starting transfers between devices, shifted(): lax.ppermute(value, axis, [(source, source + steps) for source in range(l...  101 us
    all_gather x1, waiting for transfers between devices, body(): lax.all_gather(misfit.astype(jnp.bfloat16), 'gy', axis=0, tiled=True)  90 us
    dot_general x5, matrix products, apply_cols(): jnp.dot(diag_y, field.reshape(height, -1), precision=lax.Precision.HIGHES...  18 us
    dot_general x5, matrix products, apply_rows(): jnp.einsum('ij,yjs->yis', diag_x, field, precision=lax.Precision.HIGHEST,...  12.6 us
  transfers between devices with their start and end apart: 23, of which 22 were waited for; matrix products, arithmetic and copies ran while one was open for 5% of the time, Pallas kernels for 0%

commit v1 on v0

v1 whole, which is shorter than its diff:
```python
import jax
import jax.numpy as jnp
from jax import lax
from jax.experimental import pallas as pl
from jax.experimental.pallas import tpu as pltpu
from jax.sharding import Mesh, PartitionSpec as P

NUGGET = 0.3
BLK = 64
HALF = 32
N = 1024
S = 128
TILE = 256
TILES = N // TILE
BLOCKS = N // BLK
F32 = jnp.float32
BF16 = jnp.bfloat16
VMEM = pltpu.VMEM
SMEM = pltpu.SMEM


def low_lanes(shape):
    return lax.broadcasted_iota(jnp.int32, shape, len(shape) - 1) < BLK


def swap_halves(value):
    return pltpu.roll(value, BLK, axis=1)


def split_samples_kernel(noise_ref, out_ref, tmp_ref):
    for k in range(HALF):
        pair = jnp.concatenate([noise_ref[k], noise_ref[HALF + k]], axis=0).astype(F32)
        tmp_ref[pl.ds(k, S, stride=HALF), :] = pair.T
    out_ref[...] = tmp_ref[...].reshape(S, HALF, S).astype(BF16)


def split_samples(noise):
    return pl.pallas_call(
        split_samples_kernel,
        out_shape=jax.ShapeDtypeStruct((S, HALF, S), BF16),
        in_specs=[pl.BlockSpec(memory_space=VMEM)],
        out_specs=pl.BlockSpec(memory_space=VMEM),
        scratch_shapes=[VMEM((S * HALF, S), F32)],
        compiler_params=pltpu.CompilerParams(vmem_limit_bytes=32 * 1024 * 1024),
        cost_estimate=pl.CostEstimate(flops=0, bytes_accessed=2 * 1024 * 1024, transcendentals=0),
        name="split_samples",
    )(noise)


def join_samples_kernel(msg_ref, extra_ref, out_ref, tmp_ref):
    rows = msg_ref.shape[1]
    tmp_ref[...] = msg_ref[...].astype(F32).reshape(S * rows, S)
    extra = extra_ref[0]
    for k in range(rows):
        pair = tmp_ref[pl.ds(k, S, stride=rows), :].T
        for yh in range(2):
            column = extra[:, yh * rows + k : yh * rows + k + 1]
            out_ref[yh, k] = pair[yh * BLK : (yh + 1) * BLK] + column


def join_samples(msg, extra):
    rows = 16
    steps = HALF // rows
    cols = extra.reshape(2, steps, rows, BLK).transpose(1, 3, 0, 2).reshape(steps, BLK, 2 * rows)
    out = pl.pallas_call(
        join_samples_kernel,
        grid=(steps,),
        out_shape=jax.ShapeDtypeStruct((2, HALF, BLK, S), F32),
        in_specs=[
            pl.BlockSpec((S, rows, S), lambda i: (0, i, 0)),
            pl.BlockSpec((1, BLK, 2 * rows), lambda i: (i, 0, 0)),
        ],
        out_specs=pl.BlockSpec((2, rows, BLK, S), lambda i: (0, i, 0, 0)),
        scratch_shapes=[VMEM((S * rows, S), F32)],
        compiler_params=pltpu.CompilerParams(vmem_limit_bytes=32 * 1024 * 1024),
        cost_estimate=pl.CostEstimate(flops=0, bytes_accessed=3 * 1024 * 1024, transcendentals=0),
        name="join_samples",
    )(msg, cols)
    return out.reshape(BLK, BLK, S)


def build_band(band_ref, mats_ref):
    band_ref[...] = jnp.zeros_like(band_ref)
    low = low_lanes((BLK, S))
    zero = jnp.zeros((BLK, S), F32)

    def first(b):
        return mats_ref[b, :, 0:S].astype(F32)

    def second(b):
        return mats_ref[b, :, S : 2 * S].astype(F32)

    def put(row, pair, value):
        band_ref[row * BLK : (row + 1) * BLK, pair * S : (pair + 1) * S] = value.astype(BF16)

    for pair in range(BLOCKS // 2):
        even, odd = 2 * pair, 2 * pair + 1
        put(even, pair, jnp.where(low, first(even), first(odd)))
        put(odd, pair, jnp.where(low, second(odd), swap_halves(first(odd))))
        if pair > 0:
            put(even - 1, pair, jnp.where(low, swap_halves(first(even)), zero))
        if odd + 1 < BLOCKS:
            put(odd + 1, pair, jnp.where(low, zero, swap_halves(second(odd + 1))))


def sample_kernel(
    core_ref,
    coeff_ref,
    rows_ref,
    own_ref,
    other_ref,
    xmats_ref,
    ymats_ref,
    weights_ref,
    out_ref,
    xband,
    yband,
    zb,
    fb,
    uf,
    ub,
    fa,
    fc,
    mis,
    cat,
):
    core = core_ref[0]
    low = low_lanes((HALF, S))
    build_band(xband, xmats_ref)
    build_band(yband, ymats_ref)

    @pl.loop(0, 8)
    def _(gc):
        for ref, parity in ((own_ref, core), (other_ref, 1 - core)):
            row = pl.multiple_of((2 * gc + parity) * BLK, BLK)
            for pair in range(BLOCKS // 2):
                a = ref[2 * pair, gc].astype(F32)
                b = ref[2 * pair + 1, gc].astype(F32)
                cols = slice(pair * S, (pair + 1) * S)
                zb[pl.ds(row, HALF), cols] = jnp.where(low, a, swap_halves(b)).astype(BF16)
                zb[pl.ds(row + HALF, HALF), cols] = jnp.where(low, swap_halves(a), b).astype(BF16)

    def reach(t):
        return max(0, t * TILE - S), min(N, (t + 1) * TILE + S)

    def apply(source, source_b, before, target, z_coeff, scale):
        @pl.loop(0, TILES)
        def _(r):
            rows = pl.ds(pl.multiple_of(r * TILE, TILE), TILE)
            for t in range(TILES):
                lo, hi = reach(t)
                cols = slice(t * TILE, (t + 1) * TILE)
                part = jnp.dot(source_b[rows, lo:hi], xband[lo:hi, cols], preferred_element_type=F32)
                value = NUGGET * source[rows, cols].astype(F32) + part
                uf[rows, cols] = value
                ub[rows, cols] = value.astype(BF16)

        @pl.loop(0, TILES)
        def _(c):
            cols = pl.ds(pl.multiple_of(c * TILE, TILE), TILE)
            for t in range(TILES):
                lo, hi = reach(t)
                rows = slice(t * TILE, (t + 1) * TILE)
                part = jnp.dot(yband[rows, lo:hi], ub[lo:hi, cols], preferred_element_type=F32)
                value = NUGGET * uf[rows, cols] + part
                value = scale * value + z_coeff * zb[rows, cols].astype(F32)
                if before is not None:
                    value = value - before[rows, cols]
                target[rows, cols] = value
                fb[rows, cols] = value.astype(BF16)

    c = [coeff_ref[i] for i in range(6)]
    apply(zb, zb, None, fa, c[4], 2.0 * c[5])
    apply(fa, fb, None, fc, c[3] - c[5], 2.0)
    apply(fc, fb, fa, fa, c[2], 2.0)
    apply(fa, fb, fc, fc, c[1], 2.0)
    apply(fc, fb, fa, fa, c[0], 1.0)

    @pl.loop(0, S, unroll=8)
    def _(r):
        mis[pl.ds(r, 1), :] = fa[pl.ds(rows_ref[r], 1), :]

    high = mis[...].astype(BF16)
    cat[0:S, :] = high
    cat[S : 2 * S, :] = high
    cat[2 * S : 3 * S, :] = (mis[...] - high.astype(F32)).astype(BF16)

    @pl.loop(0, 8)
    def _(gc):
        row = pl.multiple_of((2 * gc + core) * BLK, BLK)
        part = jnp.dot(weights_ref[gc], cat[...], preferred_element_type=F32)
        for pair in range(BLOCKS // 2):
            cols = slice(pair * S, (pair + 1) * S)
            a = fa[pl.ds(row, HALF), cols] - part[0:HALF, cols]
            b = fa[pl.ds(row + HALF, HALF), cols] - part[HALF:BLK, cols]
            out_ref[2 * pair, gc] = jnp.where(low, a, swap_halves(b)).astype(BF16)
            out_ref[2 * pair + 1, gc] = jnp.where(low, swap_halves(a), b).astype(BF16)


def sample_all(core, coeff, rows, own, other, xmats, ymats, weights):
    smem = pl.BlockSpec(memory_space=SMEM)
    vmem = pl.BlockSpec(memory_space=VMEM)
    return pl.pallas_call(
        sample_kernel,
        out_shape=jax.ShapeDtypeStruct((16, 8, HALF, S), BF16),
        in_specs=[smem, smem, smem, vmem, vmem, vmem, vmem, vmem],
        out_specs=vmem,
        scratch_shapes=[
            VMEM((N, N), BF16),
            VMEM((N, N), BF16),
            VMEM((N, N), BF16),
            VMEM((N, N), BF16),
            VMEM((N, N), F32),
            VMEM((N, N), BF16),
            VMEM((N, N), F32),
            VMEM((N, N), F32),
            VMEM((S, N), F32),
            VMEM((3 * S, N), BF16),
        ],
        compiler_params=pltpu.CompilerParams(vmem_limit_bytes=48 * 1024 * 1024),
        cost_estimate=pl.CostEstimate(
            flops=10 * 2 * N * N * 512, bytes_accessed=5 * 1024 * 1024, transcendentals=0
        ),
        name="sample_all",
    )(core, coeff, rows, own, other, xmats, ymats, weights)


def body(noise, cheb_coeff, diag_x, couple_x, diag_y, couple_y, track_rows, track_obs, weights):
    core = lax.axis_index("core")
    block = lax.axis_index("gc") * 2 + core
    gy = ("gc", "core")
    chips = ("gx", "gc")

    kx = couple_x.astype(F32)
    empty = jnp.zeros((BLK, BLK), F32)
    xpay = jnp.concatenate([diag_x.T, kx.T, kx, empty], axis=1)
    xmats = lax.all_gather(xpay, "gx", axis=0, tiled=False).astype(BF16)

    ky = couple_y
    local = (track_rows - block * BLK).astype(BF16)
    marks = jnp.zeros((BLK, BLK), BF16).at[0:8, 0].set(local)
    w_high = weights.astype(BF16)
    w_low = (weights - w_high.astype(F32)).astype(BF16)
    ypay = jnp.concatenate([diag_y.astype(BF16), ky.T, ky, marks, w_high, w_low], axis=1)
    ymats = lax.all_gather(ypay, gy, axis=0, tiled=False)
    rows = ymats[:, 0:8, 3 * BLK].astype(jnp.int32) + BLK * jnp.arange(16, dtype=jnp.int32)[:, None]
    own_w = lax.dynamic_index_in_dim(
        ymats[:, :, 4 * BLK :].reshape(8, 2, BLK, 2 * S), core, axis=1, keepdims=False
    )
    own_w = jnp.concatenate([own_w, own_w[:, :, 0:S]], axis=2)

    sent = split_samples(noise)
    own = lax.all_to_all(sent, chips, 0, 0, tiled=True)
    other = lax.ppermute(own, "core", [(0, 1), (1, 0)])
    shape = (16, 8, HALF, S)
    result = sample_all(
        core.reshape(1).astype(jnp.int32),
        cheb_coeff,
        rows.reshape(S),
        own.reshape(shape),
        other.reshape(shape),
        xmats,
        ymats[:, :, 0 : 4 * BLK],
        own_w,
    )
    back = lax.all_to_all(result.reshape(S, HALF, S), chips, 0, 0, tiled=True)

    obs = lax.all_gather(track_obs, gy, axis=0, tiled=True)
    extra = jnp.dot(weights, obs, precision=lax.Precision.HIGHEST, preferred_element_type=F32)
    return join_samples(back, extra)


def solution(mesh):
    fine = Mesh(mesh.devices.reshape(16, 8, 2), ("gx", "gc", "core"))
    rows = ("gc", "core")
    return jax.shard_map(
        body,
        mesh=fine,
        in_specs=(
            P(rows, "gx", None),
            P(),
            P("gx", None),
            P("gx", None),
            P(rows, None),
            P(rows, None),
            P(rows),
            P(rows, "gx"),
            P(rows, None),
        ),
        out_specs=P(rows, "gx", None),
        check_vma=False,
    )
```

time: 525 us -> 180 us (0.34); the launches traced: 516 us -> 180 us
  waiting for transfers between devices: 326 us -> 30.3 us
  starting transfers between devices: 101 us -> 26.5 us
  blocking collectives: 0 us -> 71.5 us
  matrix products: 48.8 us -> 0.18 us
  Pallas kernels: 0 us -> 31.3 us
  other arithmetic: 15.5 us -> 1.98 us
  local copies, waits for them, and re-layouts: 11 us -> 4.59 us
    ppermute x22 -> x1, waiting for transfers between devices: 236 us -> 0.01 us  [body(): other = lax.ppermute(own, 'core', [(0, 1), (1, 0)])]
    ppermute x22 -> x1, starting transfers between devices: 101 us -> 2.76 us  [body(): other = lax.ppermute(own, 'core', [(0, 1), (1, 0)])]
    all_gather x1, waiting for transfers between devices: 90 us -> 0.01 us  [body(): ymats = lax.all_gather(ypay, gy, axis=0, tiled=False)]
    all_gather x0 -> x2, blocking collectives: none -> 71.5 us  [the longest x1 35.8 us: body(): xmats = lax.all_gather(xpay, 'gx', axis=0, tiled=False).astype(BF16)]
    dot_general x31 -> x1, matrix products: 48.8 us -> 0.18 us  [body(): jnp.dot(weights, obs, precision=lax.Precision.HIGHEST, preferred_element_...]
    pallas_call x0 -> x3, Pallas kernels: none -> 31.3 us  [the longest x1 26.5 us: sample_all(): pl.pallas_call(sample_kernel, out_shape=jax.ShapeDtypeStruct((16, 8, HALF...]
    all_to_all x0 -> x2, waiting for transfers between devices: none -> 30.3 us  [the longest x1 30.3 us: body(): own = lax.all_to_all(sent, chips, 0, 0, tiled=True)]
    all_to_all x0 -> x2, starting transfers between devices: none -> 23.7 us  [the longest x1 16.3 us: body(): own = lax.all_to_all(sent, chips, 0, 0, tiled=True)]
  transfers between devices with their start and end apart: 23 -> 4, of which waited for: 22 -> 1; matrix products, arithmetic and copies ran while one was open for 5% -> 3% of each run, Pallas kernels for 0% -> 0%
where the time goes in v1:
time: 180 us
  blocking collectives  71.5 us (40%)
  Pallas kernels  31.3 us (17%)
  waiting for transfers between devices  30.3 us (17%)
  starting transfers between devices  26.5 us (15%)
  between operations  13.6 us (8%)
  local copies, waits for them, and re-layouts  4.59 us (3%)
  other arithmetic  1.98 us (1%)
    all_gather x1, blocking collectives, body(): xmats = lax.all_gather(xpay, 'gx', axis=0, tiled=False).astype(BF16)  35.8 us
    all_gather x1, blocking collectives, body(): obs = lax.all_gather(track_obs, gy, axis=0, tiled=True)  35.7 us
    all_to_all x1, waiting for transfers between devices, body(): own = lax.all_to_all(sent, chips, 0, 0, tiled=True)  30.3 us
    pallas_call x1, Pallas kernels, sample_all(): pl.pallas_call(sample_kernel, out_shape=jax.ShapeDtypeStruct((16, 8, HALF...  26.5 us
    all_to_all x1, starting transfers between devices, body(): own = lax.all_to_all(sent, chips, 0, 0, tiled=True)  16.3 us
    all_to_all x1, starting transfers between devices, body(): back = lax.all_to_all(result.reshape(S, HALF, S), chips, 0, 0, tiled=True)  7.36 us
  transfers between devices with their start and end apart: 4, of which 1 were waited for; matrix products, arithmetic and copies ran while one was open for 3% of the time, Pallas kernels for 0%

profile of v1, /device:TPU:1, one launch (start us, length us, event | category | flops | bytes accessed | tf_op | source)
XLA Modules:
  0.0 180.0 jit_solution(14291174110840939929)
XLA Ops:
  6.5 1.2 copy-done
  7.8 2.4 %split_samples.1 = bf16[128,32,128]{2,1,0:T(8,128)(2,1)} custom-call(bf16[64,64,128]{2,1,0:T(8,128)(2,1)S(1)} %copy-done), custom_call_target="tpu_custom_call" | custom-call | bytes 2097152 | tf_op jit(solution)/shard_map/split_samples/pallas_call | solution.py:38
  10.2 16.3 %all-to-all-start = ((bf16[128,32,128]{2,1,0:T(8,128)(2,1)}), bf16[128,32,128]{2,1,0:T(8,128)(2,1)S(1)}, u32[]{:S(2)}, u32[]{:S(2)}) async-start(bf16[128,32,128]{2,1,0:T(8,128)(2,1)} %split_samples.1), calls=%async_computation | async-start | bytes 2097152 | tf_op jit(solution)/shard_map/all_to_all | solution.py:253
  26.6 0.1 copy.24
  26.7 0.1 copy.16
  26.9 0.7 concatenate.11
  27.7 0.1 add.24
  27.8 0.1 copy.18
  27.9 0.1 copy.19
  28.0 0.1 pad.10.clone
  28.1 30.3 %all-to-all-done = bf16[128,32,128]{2,1,0:T(8,128)(2,1)S(1)} async-done(((bf16[128,32,128]{2,1,0:T(8,128)(2,1)}), bf16[128,32,128]{2,1,0:T(8,128)(2,1)S(1)}, u32[]{:S(2)}, u32[]{:S(2)}) %all-to-all-start) | async-done | bytes 1048608 | tf_op jit(solution)/shard_map/all_to_all | solution.py:253
  58.3 2.8 %collective-permute-start = (bf16[128,32,128]{2,1,0:T(8,128)(2,1)S(1)}, bf16[128,32,128]{2,1,0:T(8,128)(2,1)S(1)}, u32[]{:S(2)}, u32[]{:S(2)}) collective-permute-start(bf16[128,32,128]{2,1,0:T(8,128)(2,1)S(1)} %all-to-all-done), channel_id=1, source_target_pairs={{0,1},{1,0},{2,3},{3,2},{4,5},{5,4},{6,7},{7,6},{8,9},{9,8},{10,11... | collective-permute-start | bytes 3145736 | tf_op jit(solution)/shard_map/ppermute | solution.py:254
  61.1 0.1 maximum_maximum_fusion
  61.2 35.8 %all-gather.1 = bf16[1024,256]{1,0:T(8,128)(2,1)S(1)} all-gather(bf16[64,256]{1,0:T(8,128)(2,1)S(1)} %maximum_maximum_fusion), channel_id=3, replica_groups=mesh['gx'=16,'gc'=8,'core'=2] {'gx'}, dimensions={0}, use_global_device_ids=true | all-gather | bytes 557056 | tf_op jit(solution)/shard_map/all_gather | solution.py:237
  97.0 1.3 fusion
  98.3 1.2 convert_reduce_fusion
  99.5 0.6 reshape.73
  100.1 0.7 add.25.rows_ref
  100.8 26.5 %sample_all.1 = bf16[16,8,32,128]{3,2,1,0:T(8,128)(2,1)} custom-call(s32[1]{0:T(128)} %bitcast.core_ref, f32[6]{0:T(128)S(1)} %copy-done.1, s32[128]{0:T(128)S(1)} %add.25.rows_ref, bf16[16,8,32,128]{3,2,1,0:T(8,128)(2,1)S(1)} %bitcast.23, bf16[16,8,32,128]{3,2,1,0:T(8,128)(2,1)S(1)} %bitcast.25, bf16[16,64,256]{2,1,0:T(8,128)(2,1)S(1)} %bitcast.24, ...), custom_call_target="tpu_custom_call" | custom-call | flops 10737418240 | bytes 5242880 | tf_op jit(solution)/shard_map/sample_all/pallas_call | solution.py:203
  127.3 7.4 %all-to-all-start.1 = ((bf16[128,32,128]{2,1,0:T(8,128)(2,1)}), bf16[128,32,128]{2,1,0:T(8,128)(2,1)S(1)}, u32[]{:S(2)}, u32[]{:S(2)}) async-start(bf16[128,32,128]{2,1,0:T(8,128)(2,1)} %bitcast.11), calls=%async_computation.1 | async-start | bytes 2097152 | tf_op jit(solution)/shard_map/all_to_all | solution.py:266
  134.7 35.7 %all_gather.19 = f32[128,64]{1,0:T(8,128)S(1)} all-gather(f32[8,64]{1,0:T(8,128)S(1)} %copy-done.8), channel_id=1, replica_groups=mesh['gx'=16,'gc'=8,'core'=2] {'gc','core'}, dimensions={0}, use_global_device_ids=true | all-gather | bytes 34816 | tf_op jit(solution)/shard_map/all_gather | solution.py:268
  170.4 0.2 fusion.1
  170.6 0.1 copy.22.extra_ref
  170.7 2.4 %join_samples.1 = f32[2,32,64,128]{3,2,1,0:T(8,128)} custom-call(bf16[128,32,128]{2,1,0:T(8,128)(2,1)S(1)} %all-to-all-done.1.msg_ref, f32[2,64,32]{2,1,0:T(8,128)S(1)} %copy.22.extra_ref), custom_call_target="tpu_custom_call" | custom-call | bytes 3145728 | tf_op jit(solution)/shard_map/join_samples/pallas_call | solution.py:65
  (35 shorter events, 0.3 us)
Async XLA Ops:
  6.5 1.2 copy-start
  7.8 18.8 %copy-start.9 = (s32[8]{0:T(128)S(1)}, s32[8]{0:T(128)}, u32[]{:S(2)}) copy-start(s32[8]{0:T(128)} %param.17) | copy-start | bytes 100
  7.8 19.0 %copy-start.4 = (bf16[64,64]{1,0:T(8,128)(2,1)S(1)}, bf16[64,64]{1,0:T(8,128)(2,1)}, u32[]{:S(2)}) copy-start(bf16[64,64]{1,0:T(8,128)(2,1)} %param.16) | copy-start | bytes 24580
  7.8 19.0 %copy-start.6 = (f32[64,64]{1,0:T(8,128)S(1)}, f32[64,64]{1,0:T(8,128)}, u32[]{:S(2)}) copy-start(f32[64,64]{1,0:T(8,128)} %param.15) | copy-start | bytes 49156
  7.8 19.1 %copy-start.2 = (f32[64,128]{1,0:T(8,128)S(1)}, f32[64,128]{1,0:T(8,128)}, u32[]{:S(2)}) copy-start(f32[64,128]{1,0:T(8,128)} %param.19) | copy-start | bytes 98308
  7.8 20.0 %copy-start.7 = (f32[64,64]{1,0:T(8,128)S(1)}, f32[64,64]{1,0:T(8,128)}, u32[]{:S(2)}) copy-start(f32[64,64]{1,0:T(8,128)} %param.13) | copy-start | bytes 49156
  7.8 20.1 %copy-start.5 = (bf16[64,64]{1,0:T(8,128)(2,1)S(1)}, bf16[64,64]{1,0:T(8,128)(2,1)}, u32[]{:S(2)}) copy-start(bf16[64,64]{1,0:T(8,128)(2,1)} %param.14) | copy-start | bytes 24580
  10.2 48.1 %all-to-all-start = ((bf16[128,32,128]{2,1,0:T(8,128)(2,1)}), bf16[128,32,128]{2,1,0:T(8,128)(2,1)S(1)}, u32[]{:S(2)}, u32[]{:S(2)}) async-start(bf16[128,32,128]{2,1,0:T(8,128)(2,1)} %split_samples.1), calls=%async_computation | async-start | bytes 2097152 | tf_op jit(solution)/shard_map/all_to_all | solution.py:253
  26.5 70.4 %all-gather.4.cloned.1.call-start = ((), (), s32[]{:S(2)}) async-start(), calls=%async_computation.2 | async-start | bytes 1114112 | tf_op jit(solution)/shard_map/all_gather | solution.py:245
  58.3 42.5 %collective-permute-start = (bf16[128,32,128]{2,1,0:T(8,128)(2,1)S(1)}, bf16[128,32,128]{2,1,0:T(8,128)(2,1)S(1)}, u32[]{:S(2)}, u32[]{:S(2)}) collective-permute-start(bf16[128,32,128]{2,1,0:T(8,128)(2,1)S(1)} %all-to-all-done), channel_id=1, source_target_pairs={{0,1},{1,0},{2,3},{3,2},{4,5},{5,4},{6,7},{7,6},{8,9},{9,8},{10,11... | collective-permute-start | bytes 3145736 | tf_op jit(solution)/shard_map/ppermute | solution.py:254
  61.2 39.6 %copy-start.1 = (f32[6]{0:T(128)S(1)}, f32[6]{0:T(128)}, u32[]{:S(2)}) copy-start(f32[6]{0:T(128)} %coeff_ref.1) | copy-start | bytes 76
  127.3 7.4 %copy-start.8 = (f32[8,64]{1,0:T(8,128)S(1)}, f32[8,64]{1,0:T(8,128)}, u32[]{:S(2)}) copy-start(f32[8,64]{1,0:T(8,128)} %param.18) | copy-start | bytes 6148
  127.3 43.1 %copy-start.3 = (f32[64,128]{1,0:T(8,128)S(1)}, f32[64,128]{1,0:T(8,128)}, u32[]{:S(2)}) copy-start(f32[64,128]{1,0:T(8,128)} %param.19) | copy-start | bytes 98308
  127.3 43.4 %all-to-all-start.1 = ((bf16[128,32,128]{2,1,0:T(8,128)(2,1)}), bf16[128,32,128]{2,1,0:T(8,128)(2,1)S(1)}, u32[]{:S(2)}, u32[]{:S(2)}) async-start(bf16[128,32,128]{2,1,0:T(8,128)(2,1)} %bitcast.11), calls=%async_computation.1 | async-start | bytes 2097152 | tf_op jit(solution)/shard_map/all_to_all | solution.py:266
Sparse Core Ops, SparseCore 0:
  29.2 38.5 all-gather.3

commit v2 on v1

v2 whole, which is shorter than its diff:
```python
import functools

import jax
import jax.numpy as jnp
from jax import lax
from jax.experimental import pallas as pl
from jax.experimental.pallas import tpu as pltpu
from jax.sharding import Mesh, PartitionSpec as P

NUGGET = 0.3
BLK = 64
HALF = 32
N = 1024
S = 128
TILE = 256
TILES = N // TILE
BLOCKS = N // BLK
F32 = jnp.float32
BF16 = jnp.bfloat16
VMEM = pltpu.VMEM
SMEM = pltpu.SMEM


def low_lanes(shape):
    return lax.broadcasted_iota(jnp.int32, shape, len(shape) - 1) < BLK


def swap_halves(value):
    return pltpu.roll(value, BLK, axis=1)


def split_samples_kernel(noise_ref, out_ref, tmp_ref):
    for k in range(HALF):
        pair = jnp.concatenate([noise_ref[k], noise_ref[HALF + k]], axis=0).astype(F32)
        tmp_ref[pl.ds(k, S, stride=HALF), :] = pair.T
    out_ref[...] = tmp_ref[...].reshape(S, HALF, S).astype(BF16)


def split_samples(noise):
    return pl.pallas_call(
        split_samples_kernel,
        out_shape=jax.ShapeDtypeStruct((S, HALF, S), BF16),
        in_specs=[pl.BlockSpec(memory_space=VMEM)],
        out_specs=pl.BlockSpec(memory_space=VMEM),
        scratch_shapes=[VMEM((S * HALF, S), F32)],
        compiler_params=pltpu.CompilerParams(vmem_limit_bytes=32 * 1024 * 1024),
        cost_estimate=pl.CostEstimate(flops=0, bytes_accessed=2 * 1024 * 1024, transcendentals=0),
        name="split_samples",
    )(noise)


def join_samples_kernel(msg_ref, extra_ref, out_ref, tmp_ref):
    rows = msg_ref.shape[1]
    tmp_ref[...] = msg_ref[...].astype(F32).reshape(S * rows, S)
    extra = extra_ref[0]
    for k in range(rows):
        pair = tmp_ref[pl.ds(k, S, stride=rows), :].T
        for yh in range(2):
            column = extra[:, yh * rows + k : yh * rows + k + 1]
            out_ref[yh, k] = pair[yh * BLK : (yh + 1) * BLK] + column


def join_samples(msg, extra):
    rows = 16
    steps = HALF // rows
    cols = extra.reshape(2, steps, rows, BLK).transpose(1, 3, 0, 2).reshape(steps, BLK, 2 * rows)
    out = pl.pallas_call(
        join_samples_kernel,
        grid=(steps,),
        out_shape=jax.ShapeDtypeStruct((2, HALF, BLK, S), F32),
        in_specs=[
            pl.BlockSpec((S, rows, S), lambda i: (0, i, 0)),
            pl.BlockSpec((1, BLK, 2 * rows), lambda i: (i, 0, 0)),
        ],
        out_specs=pl.BlockSpec((2, rows, BLK, S), lambda i: (0, i, 0, 0)),
        scratch_shapes=[VMEM((S * rows, S), F32)],
        compiler_params=pltpu.CompilerParams(vmem_limit_bytes=32 * 1024 * 1024),
        cost_estimate=pl.CostEstimate(flops=0, bytes_accessed=3 * 1024 * 1024, transcendentals=0),
        name="join_samples",
    )(msg, cols)
    return out.reshape(BLK, BLK, S)


def payload_kernel(
    block_ref, track_ref, dx_ref, kx_ref, dy_ref, ky_ref, weights_ref, obs_ref, x_ref, y_ref
):
    x_ref[...] = jnp.concatenate([dx_ref[...].T, kx_ref[...].astype(F32)], axis=1).astype(BF16)
    y_ref[:, 0:S] = jnp.concatenate([dy_ref[...], ky_ref[...].astype(F32)], axis=1).astype(BF16)
    weights = weights_ref[...]
    high = weights.astype(BF16)
    y_ref[:, S : 2 * S] = high
    y_ref[:, 2 * S : 3 * S] = (weights - high.astype(F32)).astype(BF16)
    obs = obs_ref[...]
    one = obs.astype(BF16).astype(F32)
    two = (obs - one).astype(BF16).astype(F32)
    three = obs - one - two
    row = lax.broadcasted_iota(jnp.int32, (8, BLK), 0)
    local = jnp.zeros((8, BLK), F32)
    for j in range(8):
        local = jnp.where(row == j, (track_ref[j] - block_ref[0] * BLK).astype(F32), local)
    extra = jnp.concatenate(
        [
            jnp.concatenate([one, two], axis=1),
            jnp.concatenate([three, local], axis=1),
            jnp.zeros((BLK - 16, S), F32),
        ],
        axis=0,
    )
    y_ref[:, 3 * S : 4 * S] = extra.astype(BF16)


def payloads(block, tracks, dx, kx, dy, ky, weights, obs):
    smem = pl.BlockSpec(memory_space=SMEM)
    vmem = pl.BlockSpec(memory_space=VMEM)
    return pl.pallas_call(
        payload_kernel,
        out_shape=(
            jax.ShapeDtypeStruct((BLK, S), BF16),
            jax.ShapeDtypeStruct((BLK, 4 * S), BF16),
        ),
        in_specs=[smem, smem] + [vmem] * 6,
        out_specs=(vmem, vmem),
        name="payloads",
    )(block, tracks, dx, kx, dy, ky, weights, obs)


def reach(t):
    return max(0, t * TILE - S), min(N, (t + 1) * TILE + S)


def base(t):
    return t * TILE - S


def band_kernel(transposed, place_ref, mats_ref, t_ref, e_ref, dense):
    dense[...] = jnp.zeros_like(dense)
    zero = jnp.zeros((BLK, BLK), F32)

    def put(row, pair, left, right):
        dense[row * BLK : (row + 1) * BLK, pair * S : (pair + 1) * S] = jnp.concatenate(
            [left, right], axis=1
        ).astype(BF16)

    def block(b):
        both = mats_ref[place_ref[b], :, 0:S].astype(F32)
        return both[:, 0:BLK], both[:, BLK:S], both.T[BLK:S, :]

    for pair in range(BLOCKS // 2):
        even, odd = 2 * pair, 2 * pair + 1
        d_even, k_even, back_even = block(even)
        d_odd, k_odd, back_odd = block(odd)
        put(even, pair, d_even, back_odd)
        put(odd, pair, k_odd, d_odd)
        if pair > 0:
            put(even - 1, pair, back_even, zero)
            put(even, pair - 1, zero, k_even)

    for t in range(TILES):
        lo, hi = reach(t)
        mine = slice(t * TILE, (t + 1) * TILE)
        near = slice(lo - base(t), hi - base(t))
        if transposed:
            one = dense[lo:hi, mine]
            two = jnp.dot(dense[lo:hi, lo:hi], one, preferred_element_type=F32)
        else:
            one = dense[mine, lo:hi]
            two = jnp.dot(one, dense[lo:hi, lo:hi], preferred_element_type=F32)
        two = ((2.0 * NUGGET) * one.astype(F32) + two).astype(BF16)
        if transposed:
            t_ref[t, near, :] = one
            e_ref[t, near, :] = two
        else:
            t_ref[t, :, near] = one
            e_ref[t, :, near] = two


def bands(place, mats, transposed):
    shape = (TILES, 2 * TILE, TILE) if transposed else (TILES, TILE, 2 * TILE)
    vmem = pl.BlockSpec(memory_space=VMEM)
    return pl.pallas_call(
        functools.partial(band_kernel, transposed),
        out_shape=(jax.ShapeDtypeStruct(shape, BF16),) * 2,
        in_specs=[pl.BlockSpec(memory_space=SMEM), vmem],
        out_specs=(vmem, vmem),
        scratch_shapes=[VMEM((N, N), BF16)],
        compiler_params=pltpu.CompilerParams(vmem_limit_bytes=24 * 1024 * 1024),
        cost_estimate=pl.CostEstimate(
            flops=2 * 4 * TILE * TILE * 4 * TILE, bytes_accessed=3 * 1024 * 1024, transcendentals=0
        ),
        name="x_bands" if transposed else "y_bands",
    )(place, mats)


def sample_kernel(
    core_ref,
    coeff_ref,
    rows_ref,
    own_ref,
    other_ref,
    xt_ref,
    xe_ref,
    yt_ref,
    ye_ref,
    ymats_ref,
    out_ref,
    zb,
    fb,
    uf,
    ub,
    fa,
    fc,
    mis,
    cat,
    wcat,
):
    core = core_ref[0]
    low = low_lanes((HALF, S))

    @pl.loop(0, 8)
    def _(gc):
        for ref, parity in ((own_ref, core), (other_ref, 1 - core)):
            row = pl.multiple_of((2 * gc + parity) * BLK, BLK)
            for pair in range(BLOCKS // 2):
                a = ref[2 * pair, gc].astype(F32)
                b = ref[2 * pair + 1, gc].astype(F32)
                cols = slice(pair * S, (pair + 1) * S)
                zb[pl.ds(row, HALF), cols] = jnp.where(low, a, swap_halves(b)).astype(BF16)
                zb[pl.ds(row + HALF, HALF), cols] = jnp.where(low, swap_halves(a), b).astype(BF16)

    def along_x(source, source_b, band, share):
        for t in range(TILES):
            lo, hi = reach(t)
            cols = slice(t * TILE, (t + 1) * TILE)
            matrix = band[t, lo - base(t) : hi - base(t), :]
            part = jnp.dot(source_b[:, lo:hi], matrix, preferred_element_type=F32)
            value = share * source[:, cols].astype(F32) + part
            uf[:, cols] = value
            ub[:, cols] = value.astype(BF16)

    def along_y(band, share, finish):
        for t in range(TILES):
            lo, hi = reach(t)
            rows = slice(t * TILE, (t + 1) * TILE)
            matrix = band[t, :, lo - base(t) : hi - base(t)]
            part = jnp.dot(matrix, ub[lo:hi, :], preferred_element_type=F32)
            finish(rows, share * uf[rows, :] + part)

    c = [coeff_ref[i] for i in range(6)]
    square = NUGGET * NUGGET

    def first(rows, value):
        value = 2.0 * value - zb[rows, :].astype(F32)
        fa[rows, :] = value
        fb[rows, :] = value.astype(BF16)

    def second(rows, value):
        once = fa[rows, :]
        start = zb[rows, :].astype(F32)
        twice = 2.0 * value - once
        fa[rows, :] = (c[0] - c[4]) * start + c[2] * once + (2.0 * c[4]) * twice
        odd = (c[1] - c[3] - c[5]) * start + (2.0 * (c[3] - c[5])) * once + (4.0 * c[5]) * twice
        fc[rows, :] = odd
        fb[rows, :] = odd.astype(BF16)

    def third(rows, value):
        fa[rows, :] = fa[rows, :] + value

    along_x(zb, zb, xe_ref, square)
    along_y(ye_ref, square, first)
    along_x(fa, fb, xe_ref, square)
    along_y(ye_ref, square, second)
    along_x(fc, fb, xt_ref, NUGGET)
    along_y(yt_ref, NUGGET, third)

    @pl.loop(0, S, unroll=8)
    def _(r):
        mis[pl.ds(r, 1), :] = fa[pl.ds(rows_ref[r], 1), :]

    high = mis[...].astype(BF16)
    cat[0:S, :] = high
    cat[S : 2 * S, :] = high
    cat[2 * S : 3 * S, :] = (mis[...] - high.astype(F32)).astype(BF16)
    for gc in range(8):
        w = ymats_ref[2 * gc + core, :, S : 3 * S]
        wcat[gc * BLK : (gc + 1) * BLK, 0 : 2 * S] = w
        wcat[gc * BLK : (gc + 1) * BLK, 2 * S : 3 * S] = w[:, 0:S]
    uf[0 : 8 * BLK, :] = jnp.dot(wcat[...], cat[...], preferred_element_type=F32)

    @pl.loop(0, 8)
    def _(gc):
        row = pl.multiple_of((2 * gc + core) * BLK, BLK)
        mine = pl.multiple_of(gc * BLK, BLK)
        for pair in range(BLOCKS // 2):
            cols = slice(pair * S, (pair + 1) * S)
            a = fa[pl.ds(row, HALF), cols] - uf[pl.ds(mine, HALF), cols]
            b = fa[pl.ds(row + HALF, HALF), cols] - uf[pl.ds(mine + HALF, HALF), cols]
            out_ref[2 * pair, gc] = jnp.where(low, a, swap_halves(b)).astype(BF16)
            out_ref[2 * pair + 1, gc] = jnp.where(low, swap_halves(a), b).astype(BF16)


def sample_all(core, coeff, rows, own, other, xt, xe, yt, ye, ymats):
    smem = pl.BlockSpec(memory_space=SMEM)
    vmem = pl.BlockSpec(memory_space=VMEM)
    return pl.pallas_call(
        sample_kernel,
        out_shape=jax.ShapeDtypeStruct((16, 8, HALF, S), BF16),
        in_specs=[smem, smem, smem] + [vmem] * 7,
        out_specs=vmem,
        scratch_shapes=[
            VMEM((N, N), BF16),
            VMEM((N, N), BF16),
            VMEM((N, N), F32),
            VMEM((N, N), BF16),
            VMEM((N, N), F32),
            VMEM((N, N), F32),
            VMEM((S, N), F32),
            VMEM((3 * S, N), BF16),
            VMEM((8 * BLK, 3 * S), BF16),
        ],
        compiler_params=pltpu.CompilerParams(vmem_limit_bytes=44 * 1024 * 1024),
        cost_estimate=pl.CostEstimate(
            flops=6 * 2 * N * N * 512, bytes_accessed=5 * 1024 * 1024, transcendentals=0
        ),
        name="sample_all",
    )(core, coeff, rows, own, other, xt, xe, yt, ye, ymats)


def gather_ring(value, axis):
    size = lax.axis_size(axis)
    parts = [value] + [
        lax.ppermute(value, axis, [(i, (i + step) % size) for i in range(size)])
        for step in range(1, size)
    ]
    return jnp.stack(parts)


def body(noise, cheb_coeff, diag_x, couple_x, diag_y, couple_y, track_rows, track_obs, weights):
    core = lax.axis_index("core")
    block = lax.axis_index("gc") * 2 + core
    gy = ("gc", "core")
    chips = ("zh", "x", "gc")

    xpay, ypay = payloads(
        block.reshape(1).astype(jnp.int32),
        track_rows,
        diag_x,
        couple_x,
        diag_y,
        couple_y,
        weights,
        track_obs,
    )
    noise, xpay, ypay = lax.optimization_barrier((noise, xpay, ypay))
    ymats = lax.all_gather(ypay, gy, axis=0, tiled=False)
    sent = split_samples(noise)
    own = lax.all_to_all(sent, chips, 0, 0, tiled=True)

    xmats = gather_ring(gather_ring(xpay, "x"), "zh").reshape(16, BLK, S)
    index = jnp.arange(16, dtype=jnp.int32)
    far = (lax.axis_index("zh") - index // 4) % 4
    near = (lax.axis_index("x") - index % 4) % 4
    xt, xe = bands(far * 4 + near, xmats, True)
    yt, ye = bands(index, ymats, False)
    rows = ymats[:, 8:16, 3 * S + BLK].astype(jnp.int32) + BLK * index[:, None]
    rows = rows.reshape(S)
    own, xt, xe, yt, ye, rows = lax.optimization_barrier((own, xt, xe, yt, ye, rows))

    other = lax.ppermute(own, "core", [(0, 1), (1, 0)])
    shape = (16, 8, HALF, S)
    result = sample_all(
        core.reshape(1).astype(jnp.int32),
        cheb_coeff,
        rows,
        own.reshape(shape),
        other.reshape(shape),
        xt,
        xe,
        yt,
        ye,
        ymats,
    )
    back = lax.all_to_all(result.reshape(S, HALF, S), chips, 0, 0, tiled=True)

    parts = ymats[:, 0:16, 3 * S : 4 * S].astype(F32)
    obs = parts[:, 0:8, 0:BLK] + parts[:, 0:8, BLK:S] + parts[:, 8:16, 0:BLK]
    extra = jnp.dot(
        weights,
        obs.reshape(S, BLK),
        precision=lax.Precision.HIGHEST,
        preferred_element_type=F32,
    )
    return join_samples(back, extra)


def solution(mesh):
    fine = Mesh(mesh.devices.reshape(4, 4, 8, 2), ("zh", "x", "gc", "core"))
    rows = ("gc", "core")
    cols = ("zh", "x")
    return jax.shard_map(
        body,
        mesh=fine,
        in_specs=(
            P(rows, cols, None),
            P(),
            P(cols, None),
            P(cols, None),
            P(rows, None),
            P(rows, None),
            P(rows),
            P(rows, cols),
            P(rows, None),
        ),
        out_specs=P(rows, cols, None),
        check_vma=False,
    )
```

time: 180 us -> 142 us (0.79)
  blocking collectives: 71.5 us -> 0 us
  waiting for transfers between devices: 30.3 us -> 53.1 us
  starting transfers between devices: 26.5 us -> 41.1 us
  Pallas kernels: 31.3 us -> 22.5 us
  local copies, waits for them, and re-layouts: 4.59 us -> 8.49 us
    all_gather x2 -> x0, blocking collectives: 71.5 us -> none  [the longest x1 35.8 us: body(): xmats = lax.all_gather(xpay, 'gx', axis=0, tiled=False).astype(BF16)]
    all_to_all x1, waiting for transfers between devices: 30.3 us -> 0.01 us  [body(): own = lax.all_to_all(sent, chips, 0, 0, tiled=True)]
    all_to_all x1, waiting for transfers between devices: 0.01 us -> 28.9 us  [body(): back = lax.all_to_all(result.reshape(S, HALF, S), chips, 0, 0, tiled=True)]
    ppermute x0 -> x6, waiting for transfers between devices: none -> 21.9 us  [gather_ring(): lax.ppermute(value, axis, [(i, (i + step) % size) for i in range(size)])]
    ppermute x0 -> x6, starting transfers between devices: none -> 13.7 us  [gather_ring(): lax.ppermute(value, axis, [(i, (i + step) % size) for i in range(size)])]
    pallas_call x1, Pallas kernels: 26.5 us -> 13 us  [sample_all(): pl.pallas_call(sample_kernel, out_shape=jax.ShapeDtypeStruct((16, 8, HALF...]
    unnamed x23 -> x20, local copies, waits for them, and re-layouts: 1.53 us -> 8.07 us
    pallas_call x0 -> x3, Pallas kernels: none -> 4.63 us  [the longest x2 3.08 us: bands(): pl.pallas_call(functools.partial(band_kernel, transposed), out_shape=(jax...]
  transfers between devices with their start and end apart: 4 -> 10, of which waited for: 1 -> 6; matrix products, arithmetic and copies ran while one was open for 3% -> 2% of each run, Pallas kernels for 0% -> 4%
where the time goes in v2:
time: 142 us; the launch traced here: 141 us
  waiting for transfers between devices  53.1 us (37%)
  starting transfers between devices  41.1 us (29%)
  Pallas kernels  22.5 us (16%)
  between operations  13.6 us (10%)
  local copies, waits for them, and re-layouts  8.49 us (6%)
  other arithmetic  2.1 us (1%)
    all_to_all x1, waiting for transfers between devices, body(): back = lax.all_to_all(result.reshape(S, HALF, S), chips, 0, 0, tiled=True)  28.9 us
    ppermute x6, waiting for transfers between devices, gather_ring(): lax.ppermute(value, axis, [(i, (i + step) % size) for i in range(size)])  21.9 us
    all_to_all x1, starting transfers between devices, body(): own = lax.all_to_all(sent, chips, 0, 0, tiled=True)  16.3 us
    ppermute x6, starting transfers between devices, gather_ring(): lax.ppermute(value, axis, [(i, (i + step) % size) for i in range(size)])  13.7 us
    pallas_call x1, Pallas kernels, sample_all(): pl.pallas_call(sample_kernel, out_shape=jax.ShapeDtypeStruct((16, 8, HALF...  13 us
    all_to_all x1, starting transfers between devices, body(): back = lax.all_to_all(result.reshape(S, HALF, S), chips, 0, 0, tiled=True)  8.76 us
    unnamed x20, local copies, waits for them, and re-layouts  8.07 us
    pallas_call x2, Pallas kernels, bands(): pl.pallas_call(functools.partial(band_kernel, transposed), out_shape=(jax...  3.08 us
  transfers between devices with their start and end apart: 10, of which 6 were waited for; matrix products, arithmetic and copies ran while one was open for 2% of the time, Pallas kernels for 4%

profile of v2, /device:TPU:1, one launch (start us, length us, event | category | flops | bytes accessed | tf_op | source)
XLA Modules:
  0.0 141.2 jit_solution(8033290831989238781)
XLA Ops:
  6.5 1.6 %payloads.1 = (bf16[64,128]{1,0:T(8,128)(2,1)}, bf16[64,512]{1,0:T(8,128)(2,1)}) custom-call(s32[1]{0:T(128)} %bitcast.1.block_ref, s32[8]{0:T(128)} %track_ref.1, f32[64,64]{1,0:T(8,128)} %dx_ref.1, bf16[64,64]{1,0:T(8,128)(2,1)} %kx_ref.1, f32[64,64]{1,0:T(8,128)} %dy_ref.1, bf16[64,64]{1,0:T(8,128)(2,1)} %ky_ref.1, f32[64,128]{1,0:T(8,128)} %weights_ref.1, ...), custom_call_target="tpu_custom_call" | custom-call | tf_op jit(solution)/shard_map/payloads/pallas_call | solution.py:115
  8.1 1.2 copy-done
  9.3 2.4 %split_samples.1 = bf16[128,32,128]{2,1,0:T(8,128)(2,1)} custom-call(bf16[64,64,128]{2,1,0:T(8,128)(2,1)S(1)} %copy-done), custom_call_target="tpu_custom_call" | custom-call | bytes 2097152 | tf_op jit(solution)/shard_map/split_samples/pallas_call | solution.py:40
  11.8 16.3 %all-to-all-start = ((bf16[128,32,128]{2,1,0:T(8,128)(2,1)}), bf16[128,32,128]{2,1,0:T(8,128)(2,1)S(1)}, u32[]{:S(2)}, u32[]{:S(2)}) async-start(bf16[128,32,128]{2,1,0:T(8,128)(2,1)} %split_samples.1), calls=%async_computation | async-start | bytes 2097152 | tf_op jit(solution)/shard_map/all_to_all | solution.py:356
  28.8 2.4 %collective-permute-start.1 = (bf16[64,128]{1,0:T(8,128)(2,1)S(1)}, bf16[64,128]{1,0:T(8,128)(2,1)S(1)}, u32[]{:S(2)}, u32[]{:S(2)}) collective-permute-start(bf16[64,128]{1,0:T(8,128)(2,1)S(1)} %copy-done.9), channel_id=1, source_target_pairs={{0,32},{16,48},{32,0},{48,16},{1,33},{17,49},{33,1},{49,17},{2,34}... | collective-permute-start | bytes 49160 | tf_op jit(solution)/shard_map/ppermute | solution.py:331
  31.2 1.1 collective-permute-start.2
  34.2 2.8 %collective-permute-start.3 = (bf16[4,64,128]{2,1,0:T(8,128)(2,1)S(1)}, bf16[4,64,128]{2,1,0:T(8,128)(2,1)S(1)}, u32[]{:S(2)}, u32[]{:S(2)}) collective-permute-start(bf16[4,64,128]{2,1,0:T(8,128)(2,1)S(1)} %get-tuple-element.36), channel_id=1, source_target_pairs={{0,64},{64,128},{128,192},{192,0},{1,65},{65,129},{129,193},{193,1... | collective-permute-start | bytes 196616 | tf_op jit(solution)/shard_map/ppermute | solution.py:331
  37.0 3.4 %collective-permute-start.4 = (bf16[4,64,128]{2,1,0:T(8,128)(2,1)S(1)}, bf16[4,64,128]{2,1,0:T(8,128)(2,1)S(1)}, u32[]{:S(2)}, u32[]{:S(2)}) collective-permute-start(bf16[4,64,128]{2,1,0:T(8,128)(2,1)S(1)} %get-tuple-element.36), channel_id=1, source_target_pairs={{0,128},{64,192},{128,0},{192,64},{1,129},{65,193},{129,1},{193,65... | collective-permute-start | bytes 196616 | tf_op jit(solution)/shard_map/ppermute | solution.py:331
  40.5 3.2 %collective-permute-start.5 = (bf16[4,64,128]{2,1,0:T(8,128)(2,1)S(1)}, bf16[4,64,128]{2,1,0:T(8,128)(2,1)S(1)}, u32[]{:S(2)}, u32[]{:S(2)}) collective-permute-start(bf16[4,64,128]{2,1,0:T(8,128)(2,1)S(1)} %get-tuple-element.36), channel_id=1, source_target_pairs={{0,192},{64,0},{128,64},{192,128},{1,193},{65,1},{129,65},{193,129... | collective-permute-start | bytes 196616 | tf_op jit(solution)/shard_map/ppermute | solution.py:331
  43.7 16.8 %collective-permute-done.3 = bf16[4,64,128]{2,1,0:T(8,128)(2,1)S(1)} collective-permute-done((bf16[4,64,128]{2,1,0:T(8,128)(2,1)S(1)}, bf16[4,64,128]{2,1,0:T(8,128)(2,1)S(1)}, u32[]{:S(2)}, u32[]{:S(2)}) %collective-permute-start.3) | collective-permute-done | bytes 65568 | tf_op jit(solution)/shard_map/ppermute | solution.py:331
  60.5 3.4 %collective-permute-done.4 = bf16[4,64,128]{2,1,0:T(8,128)(2,1)S(1)} collective-permute-done((bf16[4,64,128]{2,1,0:T(8,128)(2,1)S(1)}, bf16[4,64,128]{2,1,0:T(8,128)(2,1)S(1)}, u32[]{:S(2)}, u32[]{:S(2)}) %collective-permute-start.4) | collective-permute-done | bytes 65568 | tf_op jit(solution)/shard_map/ppermute | solution.py:331
  64.0 1.5 %x_bands.1 = (bf16[4,512,256]{2,1,0:T(8,128)(2,1)S(1)}, bf16[4,512,256]{2,1,0:T(8,128)(2,1)S(1)}) custom-call(s32[16]{0:T(128)S(1)} %fusion.4.place_ref, bf16[16,64,128]{2,1,0:T(8,128)(2,1)S(1)} %bitcast.28), custom_call_target="tpu_custom_call" | custom-call | flops 536870912 | bytes 3145728 | tf_op jit(solution)/shard_map/x_bands/pallas_call | solution.py:180
  67.5 1.2 convert_reduce_fusion
  68.8 1.2 copy-done.1
  70.0 1.5 %y_bands.1 = (bf16[4,256,512]{2,1,0:T(8,128)(2,1)S(1)}, bf16[4,256,512]{2,1,0:T(8,128)(2,1)S(1)}) custom-call(s32[16]{0:T(128)S(1)} %iota.12.place_ref, bf16[16,64,512]{2,1,0:T(8,128)(2,1)S(1)} %bitcast.31), custom_call_target="tpu_custom_call" | custom-call | flops 536870912 | bytes 3145728 | tf_op jit(solution)/shard_map/y_bands/pallas_call | solution.py:180
  71.6 2.3 %collective-permute-start.6 = (bf16[128,32,128]{2,1,0:T(8,128)(2,1)S(1)}, bf16[128,32,128]{2,1,0:T(8,128)(2,1)S(1)}, u32[]{:S(2)}, u32[]{:S(2)}) collective-permute-start(bf16[128,32,128]{2,1,0:T(8,128)(2,1)S(1)} %all-to-all-done), channel_id=1, source_target_pairs={{0,1},{1,0},{2,3},{3,2},{4,5},{5,4},{6,7},{7,6},{8,9},{9,8},{10,11... | collective-permute-start | bytes 3145736 | tf_op jit(solution)/shard_map/ppermute | solution.py:368
  73.9 2.3 %collective-permute-done.6 = bf16[128,32,128]{2,1,0:T(8,128)(2,1)S(1)} collective-permute-done((bf16[128,32,128]{2,1,0:T(8,128)(2,1)S(1)}, bf16[128,32,128]{2,1,0:T(8,128)(2,1)S(1)}, u32[]{:S(2)}, u32[]{:S(2)}) %collective-permute-start.6) | collective-permute-done | bytes 1048608 | tf_op jit(solution)/shard_map/ppermute | solution.py:368
  76.2 1.2 copy-done.2
  77.4 1.2 copy-done.5
  78.6 1.2 copy-done.7
  79.9 13.0 %sample_all.1 = bf16[16,8,32,128]{3,2,1,0:T(8,128)(2,1)} custom-call(s32[1]{0:T(128)} %bitcast.core_ref, f32[6]{0:T(128)S(1)} %copy-done.3, s32[128]{0:T(128)S(1)} %add.45.rows_ref, bf16[16,8,32,128]{3,2,1,0:T(8,128)(2,1)S(1)} %bitcast.27, bf16[16,8,32,128]{3,2,1,0:T(8,128)(2,1)S(1)} %bitcast.33, bf16[4,512,256]{2,1,0:T(8,128)(2,1)S(1)} %copy-done.5, ...), custom_call_target="tpu_custom_call" | custom-call | flops 6442450944 | bytes 5242880 | tf_op jit(solution)/shard_map/sample_all/pallas_call | solution.py:304
  92.9 8.8 %all-to-all-start.1 = ((bf16[128,32,128]{2,1,0:T(8,128)(2,1)}), bf16[128,32,128]{2,1,0:T(8,128)(2,1)S(1)}, u32[]{:S(2)}, u32[]{:S(2)}) async-start(bf16[128,32,128]{2,1,0:T(8,128)(2,1)} %bitcast.14), calls=%async_computation.1 | async-start | bytes 2097152 | tf_op jit(solution)/shard_map/all_to_all | solution.py:382
  103.0 28.9 %all-to-all-done.1.msg_ref = bf16[128,32,128]{2,1,0:T(8,128)(2,1)S(1)} async-done(((bf16[128,32,128]{2,1,0:T(8,128)(2,1)}), bf16[128,32,128]{2,1,0:T(8,128)(2,1)S(1)}, u32[]{:S(2)}, u32[]{:S(2)}) %all-to-all-start.1) | async-done | bytes 1048608 | tf_op jit(solution)/shard_map/all_to_all | solution.py:382
  131.9 2.4 %join_samples.1 = f32[2,32,64,128]{3,2,1,0:T(8,128)} custom-call(bf16[128,32,128]{2,1,0:T(8,128)(2,1)S(1)} %all-to-all-done.1.msg_ref, f32[2,64,32]{2,1,0:T(8,128)S(1)} %copy.13.extra_ref), custom_call_target="tpu_custom_call" | custom-call | bytes 3145728 | tf_op jit(solution)/shard_map/join_samples/pallas_call | solution.py:67
  (38 shorter events, 6.0 us)
Async XLA Ops:
  6.5 61.0 %all-gather.3.cloned.1.call-start = ((), (), s32[]{:S(2)}) async-start(), calls=%async_computation.2 | async-start | bytes 1114112 | tf_op jit(solution)/shard_map/all_gather | solution.py:354
  8.1 1.2 copy-start
  9.3 18.8 %copy-start.9 = (bf16[64,128]{1,0:T(8,128)(2,1)S(1)}, bf16[64,128]{1,0:T(8,128)(2,1)}, u32[]{:S(2)}) copy-start(bf16[64,128]{1,0:T(8,128)(2,1)} %get-tuple-element.23) | copy-start | bytes 49156
  11.8 59.8 %all-to-all-start = ((bf16[128,32,128]{2,1,0:T(8,128)(2,1)}), bf16[128,32,128]{2,1,0:T(8,128)(2,1)S(1)}, u32[]{:S(2)}, u32[]{:S(2)}) async-start(bf16[128,32,128]{2,1,0:T(8,128)(2,1)} %split_samples.1), calls=%async_computation | async-start | bytes 2097152 | tf_op jit(solution)/shard_map/all_to_all | solution.py:356
  28.1 4.4 %collective-permute-start = (bf16[64,128]{1,0:T(8,128)(2,1)S(1)}, bf16[64,128]{1,0:T(8,128)(2,1)S(1)}, u32[]{:S(2)}, u32[]{:S(2)}) collective-permute-start(bf16[64,128]{1,0:T(8,128)(2,1)S(1)} %copy-done.9), channel_id=1, source_target_pairs={{0,16},{16,32},{32,48},{48,0},{1,17},{17,33},{33,49},{49,1},{2,18}... | collective-permute-start | bytes 49160 | tf_op jit(solution)/shard_map/ppermute | solution.py:331
  28.8 4.6 %collective-permute-start.1 = (bf16[64,128]{1,0:T(8,128)(2,1)S(1)}, bf16[64,128]{1,0:T(8,128)(2,1)S(1)}, u32[]{:S(2)}, u32[]{:S(2)}) collective-permute-start(bf16[64,128]{1,0:T(8,128)(2,1)S(1)} %copy-done.9), channel_id=1, source_target_pairs={{0,32},{16,48},{32,0},{48,16},{1,33},{17,49},{33,1},{49,17},{2,34}... | collective-permute-start | bytes 49160 | tf_op jit(solution)/shard_map/ppermute | solution.py:331
  31.2 3.0 %collective-permute-start.2 = (bf16[64,128]{1,0:T(8,128)(2,1)S(1)}, bf16[64,128]{1,0:T(8,128)(2,1)S(1)}, u32[]{:S(2)}, u32[]{:S(2)}) collective-permute-start(bf16[64,128]{1,0:T(8,128)(2,1)S(1)} %copy-done.9), channel_id=1, source_target_pairs={{0,48},{16,0},{32,16},{48,32},{1,49},{17,1},{33,17},{49,33},{2,50}... | collective-permute-start | bytes 49160 | tf_op jit(solution)/shard_map/ppermute | solution.py:331
  34.2 26.3 %collective-permute-start.3 = (bf16[4,64,128]{2,1,0:T(8,128)(2,1)S(1)}, bf16[4,64,128]{2,1,0:T(8,128)(2,1)S(1)}, u32[]{:S(2)}, u32[]{:S(2)}) collective-permute-start(bf16[4,64,128]{2,1,0:T(8,128)(2,1)S(1)} %get-tuple-element.36), channel_id=1, source_target_pairs={{0,64},{64,128},{128,192},{192,0},{1,65},{65,129},{129,193},{193,1... | collective-permute-start | bytes 196616 | tf_op jit(solution)/shard_map/ppermute | solution.py:331
  37.0 26.9 %collective-permute-start.4 = (bf16[4,64,128]{2,1,0:T(8,128)(2,1)S(1)}, bf16[4,64,128]{2,1,0:T(8,128)(2,1)S(1)}, u32[]{:S(2)}, u32[]{:S(2)}) collective-permute-start(bf16[4,64,128]{2,1,0:T(8,128)(2,1)S(1)} %get-tuple-element.36), channel_id=1, source_target_pairs={{0,128},{64,192},{128,0},{192,64},{1,129},{65,193},{129,1},{193,65... | collective-permute-start | bytes 196616 | tf_op jit(solution)/shard_map/ppermute | solution.py:331
  40.5 23.5 %collective-permute-start.5 = (bf16[4,64,128]{2,1,0:T(8,128)(2,1)S(1)}, bf16[4,64,128]{2,1,0:T(8,128)(2,1)S(1)}, u32[]{:S(2)}, u32[]{:S(2)}) collective-permute-start(bf16[4,64,128]{2,1,0:T(8,128)(2,1)S(1)} %get-tuple-element.36), channel_id=1, source_target_pairs={{0,192},{64,0},{128,64},{192,128},{1,193},{65,1},{129,65},{193,129... | collective-permute-start | bytes 196616 | tf_op jit(solution)/shard_map/ppermute | solution.py:331
  64.0 12.2 %copy-start.3 = (f32[6]{0:T(128)S(1)}, f32[6]{0:T(128)}, u32[]{:S(2)}) copy-start(f32[6]{0:T(128)} %coeff_ref.1) | copy-start | bytes 76
  65.5 1.0 copy-start.4
  66.5 1.0 copy-start.6
  68.8 1.2 copy-start.1
  71.6 4.6 %collective-permute-start.6 = (bf16[128,32,128]{2,1,0:T(8,128)(2,1)S(1)}, bf16[128,32,128]{2,1,0:T(8,128)(2,1)S(1)}, u32[]{:S(2)}, u32[]{:S(2)}) collective-permute-start(bf16[128,32,128]{2,1,0:T(8,128)(2,1)S(1)} %all-to-all-done), channel_id=1, source_target_pairs={{0,1},{1,0},{2,3},{3,2},{4,5},{5,4},{6,7},{7,6},{8,9},{9,8},{10,11... | collective-permute-start | bytes 3145736 | tf_op jit(solution)/shard_map/ppermute | solution.py:368
  76.2 1.2 copy-start.2
  77.4 1.2 copy-start.5
  78.6 1.2 copy-start.7
  92.9 9.6 %copy-start.8 = (f32[64,128]{1,0:T(8,128)S(1)}, f32[64,128]{1,0:T(8,128)}, u32[]{:S(2)}) copy-start(f32[64,128]{1,0:T(8,128)} %weights_ref.1) | copy-start | bytes 98308
  92.9 39.0 %all-to-all-start.1 = ((bf16[128,32,128]{2,1,0:T(8,128)(2,1)}), bf16[128,32,128]{2,1,0:T(8,128)(2,1)S(1)}, u32[]{:S(2)}, u32[]{:S(2)}) async-start(bf16[128,32,128]{2,1,0:T(8,128)(2,1)} %bitcast.14), calls=%async_computation.1 | async-start | bytes 2097152 | tf_op jit(solution)/shard_map/all_to_all | solution.py:382
Sparse Core Ops, SparseCore 0:
  9.2 42.8 all-gather.2

commit v3 on v2

--- a/solution.py
+++ b/solution.py
@@ -30,23 +30,26 @@
 
 
 def split_samples_kernel(noise_ref, out_ref, tmp_ref):
-    for k in range(HALF):
-        pair = jnp.concatenate([noise_ref[k], noise_ref[HALF + k]], axis=0).astype(F32)
-        tmp_ref[pl.ds(k, S, stride=HALF), :] = pair.T
-    out_ref[...] = tmp_ref[...].reshape(S, HALF, S).astype(BF16)
+    rows = out_ref.shape[1]
+    for k in range(rows):
+        pair = jnp.concatenate([noise_ref[0, k], noise_ref[1, k]], axis=0).astype(F32)
+        tmp_ref[pl.ds(k, S, stride=rows), :] = pair.T
+    out_ref[...] = tmp_ref[...].reshape(S, rows, S).astype(BF16)
 
 
 def split_samples(noise):
+    rows = 16
     return pl.pallas_call(
         split_samples_kernel,
+        grid=(HALF // rows,),
         out_shape=jax.ShapeDtypeStruct((S, HALF, S), BF16),
-        in_specs=[pl.BlockSpec(memory_space=VMEM)],
-        out_specs=pl.BlockSpec(memory_space=VMEM),
-        scratch_shapes=[VMEM((S * HALF, S), F32)],
-        compiler_params=pltpu.CompilerParams(vmem_limit_bytes=32 * 1024 * 1024),
+        in_specs=[pl.BlockSpec((2, rows, BLK, S), lambda i: (0, i, 0, 0))],
+        out_specs=pl.BlockSpec((S, rows, S), lambda i: (0, i, 0)),
+        scratch_shapes=[VMEM((S * rows, S), F32)],
+        compiler_params=pltpu.CompilerParams(vmem_limit_bytes=16 * 1024 * 1024),
         cost_estimate=pl.CostEstimate(flops=0, bytes_accessed=2 * 1024 * 1024, transcendentals=0),
         name="split_samples",
-    )(noise)
+    )(noise.reshape(2, HALF, BLK, S))
 
 
 def join_samples_kernel(msg_ref, extra_ref, out_ref, tmp_ref):
@@ -74,7 +77,7 @@
         ],
         out_specs=pl.BlockSpec((2, rows, BLK, S), lambda i: (0, i, 0, 0)),
         scratch_shapes=[VMEM((S * rows, S), F32)],
-        compiler_params=pltpu.CompilerParams(vmem_limit_bytes=32 * 1024 * 1024),
+        compiler_params=pltpu.CompilerParams(vmem_limit_bytes=16 * 1024 * 1024),
         cost_estimate=pl.CostEstimate(flops=0, bytes_accessed=3 * 1024 * 1024, transcendentals=0),
         name="join_samples",
     )(msg, cols)
@@ -132,7 +135,7 @@
     return t * TILE - S
 
 
-def band_kernel(transposed, place_ref, mats_ref, t_ref, e_ref, dense):
+def band_kernel(transposed, place_ref, mine_ref, theirs_ref, t_ref, e_ref, dense):
     dense[...] = jnp.zeros_like(dense)
     zero = jnp.zeros((BLK, BLK), F32)
 
@@ -142,7 +145,14 @@
         ).astype(BF16)
 
     def block(b):
-        both = mats_ref[place_ref[b], :, 0:S].astype(F32)
+        if transposed:
+            both = mine_ref[place_ref[b], :, 0:S]
+        else:
+            spot = place_ref[b // 2]
+            own = mine_ref[spot, :, 0:S].astype(F32)
+            other = theirs_ref[spot, :, 0:S].astype(F32)
+            both = jnp.where(place_ref[8] == b % 2, own, other)
+        both = both.astype(F32)
         return both[:, 0:BLK], both[:, BLK:S], both.T[BLK:S, :]
 
     for pair in range(BLOCKS // 2):
@@ -174,25 +184,25 @@
             e_ref[t, :, near] = two
 
 
-def bands(place, mats, transposed):
+def bands(place, mine, theirs, transposed):
     shape = (TILES, 2 * TILE, TILE) if transposed else (TILES, TILE, 2 * TILE)
     vmem = pl.BlockSpec(memory_space=VMEM)
     return pl.pallas_call(
         functools.partial(band_kernel, transposed),
         out_shape=(jax.ShapeDtypeStruct(shape, BF16),) * 2,
-        in_specs=[pl.BlockSpec(memory_space=SMEM), vmem],
+        in_specs=[pl.BlockSpec(memory_space=SMEM), vmem, vmem],
         out_specs=(vmem, vmem),
         scratch_shapes=[VMEM((N, N), BF16)],
-        compiler_params=pltpu.CompilerParams(vmem_limit_bytes=24 * 1024 * 1024),
+        compiler_params=pltpu.CompilerParams(vmem_limit_bytes=12 * 1024 * 1024),
         cost_estimate=pl.CostEstimate(
             flops=2 * 4 * TILE * TILE * 4 * TILE, bytes_accessed=3 * 1024 * 1024, transcendentals=0
         ),
         name="x_bands" if transposed else "y_bands",
-    )(place, mats)
+    )(place, mine, theirs)
 
 
 def sample_kernel(
-    core_ref,
+    place_ref,
     coeff_ref,
     rows_ref,
     own_ref,
@@ -201,7 +211,7 @@
     xe_ref,
     yt_ref,
     ye_ref,
-    ymats_ref,
+    ymine_ref,
     out_ref,
     zb,
     fb,
@@ -213,7 +223,7 @@
     cat,
     wcat,
 ):
-    core = core_ref[0]
+    core = place_ref[8]
     low = low_lanes((HALF, S))
 
     @pl.loop(0, 8)
@@ -272,16 +282,19 @@
     along_x(fc, fb, xt_ref, NUGGET)
     along_y(yt_ref, NUGGET, third)
 
-    @pl.loop(0, S, unroll=8)
-    def _(r):
-        mis[pl.ds(r, 1), :] = fa[pl.ds(rows_ref[r], 1), :]
+    @pl.loop(0, BLOCKS)
+    def _(b):
+        side = jnp.where(b % 2 == core, 0, S // 2)
+        for j in range(8):
+            row = b * BLK + rows_ref[side + place_ref[b // 2] * 8 + j]
+            mis[pl.ds(b * 8 + j, 1), :] = fa[pl.ds(row, 1), :]
 
     high = mis[...].astype(BF16)
     cat[0:S, :] = high
     cat[S : 2 * S, :] = high
     cat[2 * S : 3 * S, :] = (mis[...] - high.astype(F32)).astype(BF16)
     for gc in range(8):
-        w = ymats_ref[2 * gc + core, :, S : 3 * S]
+        w = ymine_ref[place_ref[gc], :, S : 3 * S]
         wcat[gc * BLK : (gc + 1) * BLK, 0 : 2 * S] = w
         wcat[gc * BLK : (gc + 1) * BLK, 2 * S : 3 * S] = w[:, 0:S]
     uf[0 : 8 * BLK, :] = jnp.dot(wcat[...], cat[...], preferred_element_type=F32)
@@ -298,7 +311,7 @@
             out_ref[2 * pair + 1, gc] = jnp.where(low, swap_halves(a), b).astype(BF16)
 
 
-def sample_all(core, coeff, rows, own, other, xt, xe, yt, ye, ymats):
+def sample_all(place, coeff, rows, own, other, xt, xe, yt, ye, ymine):
     smem = pl.BlockSpec(memory_space=SMEM)
     vmem = pl.BlockSpec(memory_space=VMEM)
     return pl.pallas_call(
@@ -317,12 +330,12 @@
             VMEM((3 * S, N), BF16),
             VMEM((8 * BLK, 3 * S), BF16),
         ],
-        compiler_params=pltpu.CompilerParams(vmem_limit_bytes=44 * 1024 * 1024),
+        compiler_params=pltpu.CompilerParams(vmem_limit_bytes=28 * 1024 * 1024),
         cost_estimate=pl.CostEstimate(
             flops=6 * 2 * N * N * 512, bytes_accessed=5 * 1024 * 1024, transcendentals=0
         ),
         name="sample_all",
-    )(core, coeff, rows, own, other, xt, xe, yt, ye, ymats)
+    )(place, coeff, rows, own, other, xt, xe, yt, ye, ymine)
 
 
 def gather_ring(value, axis):
@@ -336,12 +349,12 @@
 
 def body(noise, cheb_coeff, diag_x, couple_x, diag_y, couple_y, track_rows, track_obs, weights):
     core = lax.axis_index("core")
-    block = lax.axis_index("gc") * 2 + core
-    gy = ("gc", "core")
-    chips = ("zh", "x", "gc")
+    y = lax.axis_index("y")
+    zl = lax.axis_index("zl")
+    chips = ("zh", "x", "y", "zl")
 
     xpay, ypay = payloads(
-        block.reshape(1).astype(jnp.int32),
+        (y * 4 + zl * 2 + core).reshape(1).astype(jnp.int32),
         track_rows,
         diag_x,
         couple_x,
@@ -350,25 +363,32 @@
         weights,
         track_obs,
     )
-    noise, xpay, ypay = lax.optimization_barrier((noise, xpay, ypay))
-    ymats = lax.all_gather(ypay, gy, axis=0, tiled=False)
+    xfar = gather_ring(xpay, "zh")
+    yfar = gather_ring(ypay, "zl")
     sent = split_samples(noise)
+    sent, xfar, yfar = lax.optimization_barrier((sent, xfar, yfar))
     own = lax.all_to_all(sent, chips, 0, 0, tiled=True)
 
-    xmats = gather_ring(gather_ring(xpay, "x"), "zh").reshape(16, BLK, S)
+    xmats = gather_ring(xfar, "x").reshape(16, BLK, S)
+    ymine = gather_ring(yfar, "y").reshape(8, BLK, 4 * S)
+    ytheirs = lax.ppermute(ymine, "core", [(0, 1), (1, 0)])
+    own, xmats, ymine, ytheirs = lax.optimization_barrier((own, xmats, ymine, ytheirs))
+    other = lax.ppermute(own, "core", [(0, 1), (1, 0)])
+
     index = jnp.arange(16, dtype=jnp.int32)
+    near = (lax.axis_index("x") - index % 4) % 4
     far = (lax.axis_index("zh") - index // 4) % 4
-    near = (lax.axis_index("x") - index % 4) % 4
-    xt, xe = bands(far * 4 + near, xmats, True)
-    yt, ye = bands(index, ymats, False)
-    rows = ymats[:, 8:16, 3 * S + BLK].astype(jnp.int32) + BLK * index[:, None]
-    rows = rows.reshape(S)
-    own, xt, xe, yt, ye, rows = lax.optimization_barrier((own, xt, xe, yt, ye, rows))
-
-    other = lax.ppermute(own, "core", [(0, 1), (1, 0)])
+    xt, xe = bands(near * 4 + far, xmats, xmats[0:1], True)
+    index = jnp.arange(9, dtype=jnp.int32)
+    place = (y - index // 2) % 4 * 2 + (zl - index) % 2
+    place = jnp.where(index == 8, core, place).astype(jnp.int32)
+    yt, ye = bands(place, ymine, ytheirs, False)
+    extras = jnp.stack([ymine, ytheirs])[:, :, 0:16, 3 * S : 4 * S]
+    rows = extras[:, :, 8:16, BLK].astype(jnp.int32).reshape(S)
+
     shape = (16, 8, HALF, S)
     result = sample_all(
-        core.reshape(1).astype(jnp.int32),
+        place,
         cheb_coeff,
         rows,
         own.reshape(shape),
@@ -377,12 +397,17 @@
         xe,
         yt,
         ye,
-        ymats,
+        ymine,
     )
     back = lax.all_to_all(result.reshape(S, HALF, S), chips, 0, 0, tiled=True)
 
-    parts = ymats[:, 0:16, 3 * S : 4 * S].astype(F32)
-    obs = parts[:, 0:8, 0:BLK] + parts[:, 0:8, BLK:S] + parts[:, 8:16, 0:BLK]
+    parts = extras.astype(F32)
+    obs = parts[:, :, 0:8, 0:BLK] + parts[:, :, 0:8, BLK:S] + parts[:, :, 8:16, 0:BLK]
+    block = jnp.arange(16, dtype=jnp.int32)
+    spot = (y - block // 4) % 4 * 2 + (zl - block // 2) % 2
+    spot = jnp.where(block % 2 == core, spot, spot + 8)
+    order = (spot[:, None] == block[None, :]).astype(F32)
+    obs = jnp.dot(order, obs.reshape(16, 8 * BLK), precision=lax.Precision.HIGHEST)
     extra = jnp.dot(
         weights,
         obs.reshape(S, BLK),
@@ -393,8 +418,8 @@
 
 
 def solution(mesh):
-    fine = Mesh(mesh.devices.reshape(4, 4, 8, 2), ("zh", "x", "gc", "core"))
-    rows = ("gc", "core")
+    fine = Mesh(mesh.devices.reshape(4, 4, 4, 2, 2), ("zh", "x", "y", "zl", "core"))
+    rows = ("y", "zl", "core")
     cols = ("zh", "x")
     return jax.shard_map(
         body,

time: 142 us -> 117 us (0.82)
  between operations: 13.6 us -> 0.18 us
  local copies, waits for them, and re-layouts: 8.49 us -> 1.66 us
  waiting for transfers between devices: 53.1 us -> 49.5 us
    unnamed x20 -> x10, local copies, waits for them, and re-layouts: 8.07 us -> 1.24 us
    ppermute x6 -> x10, starting transfers between devices: 13.7 us -> 18.2 us  [gather_ring(): lax.ppermute(value, axis, [(i, (i + step) % size) for i in range(size)])]
    all_to_all x1, starting transfers between devices: 16.3 us -> 11.9 us  [body(): own = lax.all_to_all(sent, chips, 0, 0, tiled=True)]
    ppermute x6 -> x10, waiting for transfers between devices: 21.9 us -> 19.5 us  [gather_ring(): lax.ppermute(value, axis, [(i, (i + step) % size) for i in range(size)])]
    all_to_all x1, starting transfers between devices: 8.76 us -> 6.41 us  [body(): back = lax.all_to_all(result.reshape(S, HALF, S), chips, 0, 0, tiled=True)]
    ppermute x1, waiting for transfers between devices: 2.29 us -> 0.01 us  [body(): other = lax.ppermute(own, 'core', [(0, 1), (1, 0)])]
    ppermute x1, starting transfers between devices: 2.32 us -> 4.2 us  [body(): other = lax.ppermute(own, 'core', [(0, 1), (1, 0)])]
    convert_element_type x2, other arithmetic: 2.03 us -> 0.43 us  [the longest x1 0.42 us: body(): rows = extras[:, :, 8:16, BLK].astype(jnp.int32).reshape(S)]
  transfers between devices with their start and end apart: 10 -> 14, of which waited for: 6 -> 8; matrix products, arithmetic and copies ran while one was open for 2% -> 1% of each run, Pallas kernels for 4% -> 4%
where the time goes in v3:
time: 117 us
  waiting for transfers between devices  49.5 us (42%)
  starting transfers between devices  42.3 us (36%)
  Pallas kernels  22.1 us (19%)
  local copies, waits for them, and re-layouts  1.66 us (1%)
    all_to_all x1, waiting for transfers between devices, body(): back = lax.all_to_all(result.reshape(S, HALF, S), chips, 0, 0, tiled=True)  29.9 us
    ppermute x10, waiting for transfers between devices, gather_ring(): lax.ppermute(value, axis, [(i, (i + step) % size) for i in range(size)])  19.5 us
    ppermute x10, starting transfers between devices, gather_ring(): lax.ppermute(value, axis, [(i, (i + step) % size) for i in range(size)])  18.2 us
    pallas_call x1, Pallas kernels, sample_all(): pl.pallas_call(sample_kernel, out_shape=jax.ShapeDtypeStruct((16, 8, HALF...  13.4 us
    all_to_all x1, starting transfers between devices, body(): own = lax.all_to_all(sent, chips, 0, 0, tiled=True)  11.9 us
    all_to_all x1, starting transfers between devices, body(): back = lax.all_to_all(result.reshape(S, HALF, S), chips, 0, 0, tiled=True)  6.41 us
    ppermute x1, starting transfers between devices, body(): other = lax.ppermute(own, 'core', [(0, 1), (1, 0)])  4.2 us
    pallas_call x2, Pallas kernels, bands(): pl.pallas_call(functools.partial(band_kernel, transposed), out_shape=(jax...  3.09 us
  transfers between devices with their start and end apart: 14, of which 8 were waited for; matrix products, arithmetic and copies ran while one was open for 1% of the time, Pallas kernels for 4%

profile of v3, /device:TPU:1, one launch (start us, length us, event | category | flops | bytes accessed | tf_op | source)
XLA Modules:
  0.0 116.9 jit_solution(15265324228451901541)
XLA Ops:
  0.0 1.6 %payloads.1 = (bf16[64,128]{1,0:T(8,128)(2,1)}, bf16[64,512]{1,0:T(8,128)(2,1)}) custom-call(s32[1]{0:T(128)} %bitcast.1.block_ref, s32[8]{0:T(128)} %track_ref.1, f32[64,64]{1,0:T(8,128)} %dx_ref.1, bf16[64,64]{1,0:T(8,128)(2,1)} %kx_ref.1, f32[64,64]{1,0:T(8,128)} %dy_ref.1, bf16[64,64]{1,0:T(8,128)(2,1)} %ky_ref.1, f32[64,128]{1,0:T(8,128)} %weights_ref.1, ...), custom_call_target="tpu_custom_call" | custom-call | tf_op jit(solution)/shard_map/payloads/pallas_call | solution.py:118
  1.6 6.8 %collective-permute-start.2 = (bf16[64,128]{1,0:T(8,128)(2,1)}, bf16[64,128]{1,0:T(8,128)(2,1)S(1)}, u32[]{:S(2)}, u32[]{:S(2)}) collective-permute-start(bf16[64,128]{1,0:T(8,128)(2,1)} %get-tuple-element.18), channel_id=1, source_target_pairs={{0,192},{64,0},{128,64},{192,128},{1,193},{65,1},{129,65},{193,129... | collective-permute-start | bytes 49160 | tf_op jit(solution)/shard_map/ppermute | solution.py:344
  8.4 0.9 collective-permute-start.1
  9.3 2.4 %collective-permute-start = (bf16[64,128]{1,0:T(8,128)(2,1)}, bf16[64,128]{1,0:T(8,128)(2,1)S(1)}, u32[]{:S(2)}, u32[]{:S(2)}) collective-permute-start(bf16[64,128]{1,0:T(8,128)(2,1)} %get-tuple-element.18), channel_id=1, source_target_pairs={{0,64},{64,128},{128,192},{192,0},{1,65},{65,129},{129,193},{193,1... | collective-permute-start | bytes 49160 | tf_op jit(solution)/shard_map/ppermute | solution.py:344
  12.4 1.2 %copy-done = bf16[64,64,128]{2,1,0:T(8,128)(2,1)S(1)} copy-done((bf16[64,64,128]{2,1,0:T(8,128)(2,1)S(1)}, bf16[64,64,128]{2,1,0:T(8,128)(2,1)}, u32[]{:S(2)}) %copy-start) | copy-done | bytes 1048600
  13.6 1.7 %split_samples.1 = bf16[128,32,128]{2,1,0:T(8,128)(2,1)} custom-call(bf16[2,32,64,128]{3,2,1,0:T(8,128)(2,1)S(1)} %bitcast.42), custom_call_target="tpu_custom_call" | custom-call | bytes 2097152 | tf_op jit(solution)/shard_map/split_samples/pallas_call | solution.py:42
  15.5 11.9 %all-to-all-start = ((bf16[128,32,128]{2,1,0:T(8,128)(2,1)}), bf16[128,32,128]{2,1,0:T(8,128)(2,1)S(1)}, u32[]{:S(2)}, u32[]{:S(2)}) async-start(bf16[128,32,128]{2,1,0:T(8,128)(2,1)} %split_samples.1), calls=%async_computation | async-start | bytes 2097152 | tf_op jit(solution)/shard_map/all_to_all | solution.py:370
  27.4 1.9 %collective-permute-start.9 = (bf16[2,64,512]{2,1,0:T(8,128)(2,1)S(1)}, bf16[2,64,512]{2,1,0:T(8,128)(2,1)S(1)}, u32[]{:S(2)}, u32[]{:S(2)}) collective-permute-start(bf16[2,64,512]{2,1,0:T(8,128)(2,1)S(1)} %pad_maximum_fusion.2), channel_id=1, source_target_pairs={{0,12},{4,0},{8,4},{12,8},{1,13},{5,1},{9,5},{13,9},{2,14},{6,2},{... | collective-permute-start | bytes 393224 | tf_op jit(solution)/shard_map/ppermute | solution.py:344
  30.4 3.8 %collective-permute-done.9 = bf16[2,64,512]{2,1,0:T(8,128)(2,1)S(1)} collective-permute-done((bf16[2,64,512]{2,1,0:T(8,128)(2,1)S(1)}, bf16[2,64,512]{2,1,0:T(8,128)(2,1)S(1)}, u32[]{:S(2)}, u32[]{:S(2)}) %collective-permute-start.9) | collective-permute-done | bytes 131104 | tf_op jit(solution)/shard_map/ppermute | solution.py:344
  34.2 2.6 %collective-permute-done.8 = bf16[2,64,512]{2,1,0:T(8,128)(2,1)S(1)} collective-permute-done((bf16[2,64,512]{2,1,0:T(8,128)(2,1)S(1)}, bf16[2,64,512]{2,1,0:T(8,128)(2,1)S(1)}, u32[]{:S(2)}, u32[]{:S(2)}) %collective-permute-start.8) | collective-permute-done | bytes 131104 | tf_op jit(solution)/shard_map/ppermute | solution.py:344
  36.9 5.7 %collective-permute-done.7 = bf16[2,64,512]{2,1,0:T(8,128)(2,1)S(1)} collective-permute-done((bf16[2,64,512]{2,1,0:T(8,128)(2,1)S(1)}, bf16[2,64,512]{2,1,0:T(8,128)(2,1)S(1)}, u32[]{:S(2)}, u32[]{:S(2)}) %collective-permute-start.7) | collective-permute-done | bytes 131104 | tf_op jit(solution)/shard_map/ppermute | solution.py:344
  42.6 1.6 %collective-permute-start.10 = (bf16[8,64,512]{2,1,0:T(8,128)(2,1)S(1)}, bf16[8,64,512]{2,1,0:T(8,128)(2,1)S(1)}, u32[]{:S(2)}, u32[]{:S(2)}) collective-permute-start(bf16[8,64,512]{2,1,0:T(8,128)(2,1)S(1)} %bitcast.35), channel_id=1, source_target_pairs={{0,1},{1,0},{2,3},{3,2},{4,5},{5,4},{6,7},{7,6},{8,9},{9,8},{10,11... | collective-permute-start | bytes 1572872 | tf_op jit(solution)/shard_map/ppermute | solution.py:374
  44.2 3.2 %collective-permute-start.6 = (bf16[4,64,128]{2,1,0:T(8,128)(2,1)S(1)}, bf16[4,64,128]{2,1,0:T(8,128)(2,1)S(1)}, u32[]{:S(2)}, u32[]{:S(2)}) collective-permute-start(bf16[4,64,128]{2,1,0:T(8,128)(2,1)S(1)} %pad_maximum_fusion.4), channel_id=1, source_target_pairs={{0,48},{16,0},{32,16},{48,32},{1,49},{17,1},{33,17},{49,33},{2,50}... | collective-permute-start | bytes 196616 | tf_op jit(solution)/shard_map/ppermute | solution.py:344
  47.4 1.1 collective-permute-start.5
  48.6 2.4 %collective-permute-done.6 = bf16[4,64,128]{2,1,0:T(8,128)(2,1)S(1)} collective-permute-done((bf16[4,64,128]{2,1,0:T(8,128)(2,1)S(1)}, bf16[4,64,128]{2,1,0:T(8,128)(2,1)S(1)}, u32[]{:S(2)}, u32[]{:S(2)}) %collective-permute-start.6) | collective-permute-done | bytes 65568 | tf_op jit(solution)/shard_map/ppermute | solution.py:344
  50.9 2.7 %collective-permute-done.5 = bf16[4,64,128]{2,1,0:T(8,128)(2,1)S(1)} collective-permute-done((bf16[4,64,128]{2,1,0:T(8,128)(2,1)S(1)}, bf16[4,64,128]{2,1,0:T(8,128)(2,1)S(1)}, u32[]{:S(2)}, u32[]{:S(2)}) %collective-permute-start.5) | collective-permute-done | bytes 65568 | tf_op jit(solution)/shard_map/ppermute | solution.py:344
  53.7 2.2 %collective-permute-done.4 = bf16[4,64,128]{2,1,0:T(8,128)(2,1)S(1)} collective-permute-done((bf16[4,64,128]{2,1,0:T(8,128)(2,1)S(1)}, bf16[4,64,128]{2,1,0:T(8,128)(2,1)S(1)}, u32[]{:S(2)}, u32[]{:S(2)}) %collective-permute-start.4) | collective-permute-done | bytes 65568 | tf_op jit(solution)/shard_map/ppermute | solution.py:344
  55.9 4.2 %collective-permute-start.11 = (bf16[128,32,128]{2,1,0:T(8,128)(2,1)S(1)}, bf16[128,32,128]{2,1,0:T(8,128)(2,1)S(1)}, u32[]{:S(2)}, u32[]{:S(2)}) collective-permute-start(bf16[128,32,128]{2,1,0:T(8,128)(2,1)S(1)} %all-to-all-done), channel_id=1, source_target_pairs={{0,1},{1,0},{2,3},{3,2},{4,5},{5,4},{6,7},{7,6},{8,9},{9,8},{10,11... | collective-permute-start | bytes 3145736 | tf_op jit(solution)/shard_map/ppermute | solution.py:376
  60.7 1.6 %y_bands.1 = (bf16[4,256,512]{2,1,0:T(8,128)(2,1)S(1)}, bf16[4,256,512]{2,1,0:T(8,128)(2,1)S(1)}) custom-call(s32[9]{0:T(128)S(1)} %compare_select_fusion.13.place_ref, bf16[8,64,512]{2,1,0:T(8,128)(2,1)S(1)} %bitcast.37, bf16[8,64,512]{2,1,0:T(8,128)(2,1)S(1)} %collective-permute-done.10.theirs_ref), custom_call_target="tpu_custom_call" | custom-call | flops 536870912 | bytes 3145728 | tf_op jit(solution)/shard_map/y_bands/pallas_call | solution.py:190
  62.2 1.5 %x_bands.1 = (bf16[4,512,256]{2,1,0:T(8,128)(2,1)S(1)}, bf16[4,512,256]{2,1,0:T(8,128)(2,1)S(1)}) custom-call(s32[16]{0:T(128)S(1)} %fusion.4.place_ref, bf16[16,64,128]{2,1,0:T(8,128)(2,1)S(1)} %bitcast.45, bf16[1,64,128]{2,1,0:T(8,128)(2,1)S(1)} %slice.20.theirs_ref), custom_call_target="tpu_custom_call" | custom-call | flops 536870912 | bytes 3145728 | tf_op jit(solution)/shard_map/x_bands/pallas_call | solution.py:190
  63.8 13.4 %sample_all.1 = bf16[16,8,32,128]{3,2,1,0:T(8,128)(2,1)} custom-call(s32[9]{0:T(128)S(1)} %compare_select_fusion.13.place_ref, f32[6]{0:T(128)S(1)} %copy-done.1, s32[128]{0:T(128)S(1)} %reshape.111.rows_ref, bf16[16,8,32,128]{3,2,1,0:T(8,128)(2,1)S(1)} %bitcast.43, bf16[16,8,32,128]{3,2,1,0:T(8,128)(2,1)S(1)} %bitcast.46, ...), custom_call_target="tpu_custom_call" | custom-call | flops 6442450944 | bytes 5242880 | tf_op jit(solution)/shard_map/sample_all/pallas_call | solution.py:317
  77.2 6.4 %all-to-all-start.1 = ((bf16[128,32,128]{2,1,0:T(8,128)(2,1)}), bf16[128,32,128]{2,1,0:T(8,128)(2,1)S(1)}, u32[]{:S(2)}, u32[]{:S(2)}) async-start(bf16[128,32,128]{2,1,0:T(8,128)(2,1)} %bitcast.22), calls=%async_computation.1 | async-start | bytes 2097152 | tf_op jit(solution)/shard_map/all_to_all | solution.py:402
  84.5 29.9 %all-to-all-done.1.msg_ref = bf16[128,32,128]{2,1,0:T(8,128)(2,1)S(1)} async-done(((bf16[128,32,128]{2,1,0:T(8,128)(2,1)}), bf16[128,32,128]{2,1,0:T(8,128)(2,1)S(1)}, u32[]{:S(2)}, u32[]{:S(2)}) %all-to-all-start.1) | async-done | bytes 1048608 | tf_op jit(solution)/shard_map/all_to_all | solution.py:402
  114.4 2.4 %join_samples.1 = f32[2,32,64,128]{3,2,1,0:T(8,128)} custom-call(bf16[128,32,128]{2,1,0:T(8,128)(2,1)S(1)} %all-to-all-done.1.msg_ref, f32[2,64,32]{2,1,0:T(8,128)S(1)} %copy.13.extra_ref), custom_call_target="tpu_custom_call" | custom-call | bytes 3145728 | tf_op jit(solution)/shard_map/join_samples/pallas_call | solution.py:70
  (39 shorter events, 3.7 us)
Async XLA Ops:
  1.6 13.8 %collective-permute-start.2 = (bf16[64,128]{1,0:T(8,128)(2,1)}, bf16[64,128]{1,0:T(8,128)(2,1)S(1)}, u32[]{:S(2)}, u32[]{:S(2)}) collective-permute-start(bf16[64,128]{1,0:T(8,128)(2,1)} %get-tuple-element.18), channel_id=1, source_target_pairs={{0,192},{64,0},{128,64},{192,128},{1,193},{65,1},{129,65},{193,129... | collective-permute-start | bytes 49160 | tf_op jit(solution)/shard_map/ppermute | solution.py:344
  8.4 6.9 %collective-permute-start.1 = (bf16[64,128]{1,0:T(8,128)(2,1)}, bf16[64,128]{1,0:T(8,128)(2,1)S(1)}, u32[]{:S(2)}, u32[]{:S(2)}) collective-permute-start(bf16[64,128]{1,0:T(8,128)(2,1)} %get-tuple-element.18), channel_id=1, source_target_pairs={{0,128},{64,192},{128,0},{192,64},{1,129},{65,193},{129,1},{193,65... | collective-permute-start | bytes 49160 | tf_op jit(solution)/shard_map/ppermute | solution.py:344
  9.3 6.0 %collective-permute-start = (bf16[64,128]{1,0:T(8,128)(2,1)}, bf16[64,128]{1,0:T(8,128)(2,1)S(1)}, u32[]{:S(2)}, u32[]{:S(2)}) collective-permute-start(bf16[64,128]{1,0:T(8,128)(2,1)} %get-tuple-element.18), channel_id=1, source_target_pairs={{0,64},{64,128},{128,192},{192,0},{1,65},{65,129},{129,193},{193,1... | collective-permute-start | bytes 49160 | tf_op jit(solution)/shard_map/ppermute | solution.py:344
  11.7 3.8 %collective-permute-start.3 = (bf16[64,512]{1,0:T(8,128)(2,1)}, bf16[64,512]{1,0:T(8,128)(2,1)S(1)}, u32[]{:S(2)}, u32[]{:S(2)}) collective-permute-start(bf16[64,512]{1,0:T(8,128)(2,1)} %get-tuple-element.19), channel_id=1, source_target_pairs={{0,2},{2,0},{1,3},{3,1},{4,6},{6,4},{5,7},{7,5},{8,10},{10,8},{9,1... | collective-permute-start | bytes 196616 | tf_op jit(solution)/shard_map/ppermute | solution.py:344
  12.4 1.2 %copy-start = (bf16[64,64,128]{2,1,0:T(8,128)(2,1)S(1)}, bf16[64,64,128]{2,1,0:T(8,128)(2,1)}, u32[]{:S(2)}) copy-start(bf16[64,64,128]{2,1,0:T(8,128)(2,1)} %param.9) | copy-start | bytes 3145732
  13.6 1.7 %copy-start.4 = (bf16[64,128]{1,0:T(8,128)(2,1)S(1)}, bf16[64,128]{1,0:T(8,128)(2,1)}, u32[]{:S(2)}) copy-start(bf16[64,128]{1,0:T(8,128)(2,1)} %get-tuple-element.18) | copy-start | bytes 49156
  13.6 1.8 %copy-start.3 = (bf16[64,512]{1,0:T(8,128)(2,1)S(1)}, bf16[64,512]{1,0:T(8,128)(2,1)}, u32[]{:S(2)}) copy-start(bf16[64,512]{1,0:T(8,128)(2,1)} %get-tuple-element.19) | copy-start | bytes 196612
  15.5 40.4 %all-to-all-start = ((bf16[128,32,128]{2,1,0:T(8,128)(2,1)}), bf16[128,32,128]{2,1,0:T(8,128)(2,1)S(1)}, u32[]{:S(2)}, u32[]{:S(2)}) async-start(bf16[128,32,128]{2,1,0:T(8,128)(2,1)} %split_samples.1), calls=%async_computation | async-start | bytes 2097152 | tf_op jit(solution)/shard_map/all_to_all | solution.py:370
  27.4 6.8 %collective-permute-start.9 = (bf16[2,64,512]{2,1,0:T(8,128)(2,1)S(1)}, bf16[2,64,512]{2,1,0:T(8,128)(2,1)S(1)}, u32[]{:S(2)}, u32[]{:S(2)}) collective-permute-start(bf16[2,64,512]{2,1,0:T(8,128)(2,1)S(1)} %pad_maximum_fusion.2), channel_id=1, source_target_pairs={{0,12},{4,0},{8,4},{12,8},{1,13},{5,1},{9,5},{13,9},{2,14},{6,2},{... | collective-permute-start | bytes 393224 | tf_op jit(solution)/shard_map/ppermute | solution.py:344
  29.2 7.6 %collective-permute-start.8 = (bf16[2,64,512]{2,1,0:T(8,128)(2,1)S(1)}, bf16[2,64,512]{2,1,0:T(8,128)(2,1)S(1)}, u32[]{:S(2)}, u32[]{:S(2)}) collective-permute-start(bf16[2,64,512]{2,1,0:T(8,128)(2,1)S(1)} %pad_maximum_fusion.2), channel_id=1, source_target_pairs={{0,8},{4,12},{8,0},{12,4},{1,9},{5,13},{9,1},{13,5},{2,10},{6,14},... | collective-permute-start | bytes 393224 | tf_op jit(solution)/shard_map/ppermute | solution.py:344
  29.8 12.8 %collective-permute-start.7 = (bf16[2,64,512]{2,1,0:T(8,128)(2,1)S(1)}, bf16[2,64,512]{2,1,0:T(8,128)(2,1)S(1)}, u32[]{:S(2)}, u32[]{:S(2)}) collective-permute-start(bf16[2,64,512]{2,1,0:T(8,128)(2,1)S(1)} %pad_maximum_fusion.2), channel_id=1, source_target_pairs={{0,4},{4,8},{8,12},{12,0},{1,5},{5,9},{9,13},{13,1},{2,6},{6,10},{... | collective-permute-start | bytes 393224 | tf_op jit(solution)/shard_map/ppermute | solution.py:344
  42.6 13.2 %collective-permute-start.10 = (bf16[8,64,512]{2,1,0:T(8,128)(2,1)S(1)}, bf16[8,64,512]{2,1,0:T(8,128)(2,1)S(1)}, u32[]{:S(2)}, u32[]{:S(2)}) collective-permute-start(bf16[8,64,512]{2,1,0:T(8,128)(2,1)S(1)} %bitcast.35), channel_id=1, source_target_pairs={{0,1},{1,0},{2,3},{3,2},{4,5},{5,4},{6,7},{7,6},{8,9},{9,8},{10,11... | collective-permute-start | bytes 1572872 | tf_op jit(solution)/shard_map/ppermute | solution.py:374
  44.2 6.7 %collective-permute-start.6 = (bf16[4,64,128]{2,1,0:T(8,128)(2,1)S(1)}, bf16[4,64,128]{2,1,0:T(8,128)(2,1)S(1)}, u32[]{:S(2)}, u32[]{:S(2)}) collective-permute-start(bf16[4,64,128]{2,1,0:T(8,128)(2,1)S(1)} %pad_maximum_fusion.4), channel_id=1, source_target_pairs={{0,48},{16,0},{32,16},{48,32},{1,49},{17,1},{33,17},{49,33},{2,50}... | collective-permute-start | bytes 196616 | tf_op jit(solution)/shard_map/ppermute | solution.py:344
  47.4 6.3 %collective-permute-start.5 = (bf16[4,64,128]{2,1,0:T(8,128)(2,1)S(1)}, bf16[4,64,128]{2,1,0:T(8,128)(2,1)S(1)}, u32[]{:S(2)}, u32[]{:S(2)}) collective-permute-start(bf16[4,64,128]{2,1,0:T(8,128)(2,1)S(1)} %pad_maximum_fusion.4), channel_id=1, source_target_pairs={{0,32},{16,48},{32,0},{48,16},{1,33},{17,49},{33,1},{49,17},{2,34}... | collective-permute-start | bytes 196616 | tf_op jit(solution)/shard_map/ppermute | solution.py:344
  48.5 7.4 %collective-permute-start.4 = (bf16[4,64,128]{2,1,0:T(8,128)(2,1)S(1)}, bf16[4,64,128]{2,1,0:T(8,128)(2,1)S(1)}, u32[]{:S(2)}, u32[]{:S(2)}) collective-permute-start(bf16[4,64,128]{2,1,0:T(8,128)(2,1)S(1)} %pad_maximum_fusion.4), channel_id=1, source_target_pairs={{0,16},{16,32},{32,48},{48,0},{1,17},{17,33},{33,49},{49,1},{2,18}... | collective-permute-start | bytes 196616 | tf_op jit(solution)/shard_map/ppermute | solution.py:344
  55.9 7.9 %collective-permute-start.11 = (bf16[128,32,128]{2,1,0:T(8,128)(2,1)S(1)}, bf16[128,32,128]{2,1,0:T(8,128)(2,1)S(1)}, u32[]{:S(2)}, u32[]{:S(2)}) collective-permute-start(bf16[128,32,128]{2,1,0:T(8,128)(2,1)S(1)} %all-to-all-done), channel_id=1, source_target_pairs={{0,1},{1,0},{2,3},{3,2},{4,5},{5,4},{6,7},{7,6},{8,9},{9,8},{10,11... | collective-permute-start | bytes 3145736 | tf_op jit(solution)/shard_map/ppermute | solution.py:376
  60.6 3.2 %copy-start.1 = (f32[6]{0:T(128)S(1)}, f32[6]{0:T(128)}, u32[]{:S(2)}) copy-start(f32[6]{0:T(128)} %coeff_ref.1) | copy-start | bytes 76
  77.2 6.9 %copy-start.2 = (f32[64,128]{1,0:T(8,128)S(1)}, f32[64,128]{1,0:T(8,128)}, u32[]{:S(2)}) copy-start(f32[64,128]{1,0:T(8,128)} %weights_ref.1) | copy-start | bytes 98308
  77.2 37.3 %all-to-all-start.1 = ((bf16[128,32,128]{2,1,0:T(8,128)(2,1)}), bf16[128,32,128]{2,1,0:T(8,128)(2,1)S(1)}, u32[]{:S(2)}, u32[]{:S(2)}) async-start(bf16[128,32,128]{2,1,0:T(8,128)(2,1)} %bitcast.22), calls=%async_computation.1 | async-start | bytes 2097152 | tf_op jit(solution)/shard_map/all_to_all | solution.py:402

commit v4 on v3

--- a/solution.py
+++ b/solution.py
@@ -46,7 +46,7 @@
         in_specs=[pl.BlockSpec((2, rows, BLK, S), lambda i: (0, i, 0, 0))],
         out_specs=pl.BlockSpec((S, rows, S), lambda i: (0, i, 0)),
         scratch_shapes=[VMEM((S * rows, S), F32)],
-        compiler_params=pltpu.CompilerParams(vmem_limit_bytes=16 * 1024 * 1024),
+        compiler_params=pltpu.CompilerParams(vmem_limit_bytes=60 * 1024 * 1024),
         cost_estimate=pl.CostEstimate(flops=0, bytes_accessed=2 * 1024 * 1024, transcendentals=0),
         name="split_samples",
     )(noise.reshape(2, HALF, BLK, S))
@@ -135,7 +135,9 @@
     return t * TILE - S
 
 
-def band_kernel(transposed, place_ref, mine_ref, theirs_ref, t_ref, e_ref, dense):
+def band_kernel(
+    place_ref, x_ref, mine_ref, theirs_ref, xt_ref, xe_ref, yt_ref, ye_ref, dense
+):
     dense[...] = jnp.zeros_like(dense)
     zero = jnp.zeros((BLK, BLK), F32)
 
@@ -144,61 +146,51 @@
             [left, right], axis=1
         ).astype(BF16)
 
-    def block(b):
-        if transposed:
-            both = mine_ref[place_ref[b], :, 0:S]
-        else:
-            spot = place_ref[b // 2]
-            own = mine_ref[spot, :, 0:S].astype(F32)
-            other = theirs_ref[spot, :, 0:S].astype(F32)
-            both = jnp.where(place_ref[8] == b % 2, own, other)
-        both = both.astype(F32)
+    def x_block(b):
+        return x_ref[place_ref[16 + b], :, 0:S].astype(F32)
+
+    def y_block(b):
+        spot = place_ref[b // 2]
+        own = mine_ref[spot, :, 0:S].astype(F32)
+        other = theirs_ref[spot, :, 0:S].astype(F32)
+        return jnp.where(place_ref[8] == b % 2, own, other)
+
+    def split(both):
         return both[:, 0:BLK], both[:, BLK:S], both.T[BLK:S, :]
 
-    for pair in range(BLOCKS // 2):
-        even, odd = 2 * pair, 2 * pair + 1
-        d_even, k_even, back_even = block(even)
-        d_odd, k_odd, back_odd = block(odd)
-        put(even, pair, d_even, back_odd)
-        put(odd, pair, k_odd, d_odd)
-        if pair > 0:
-            put(even - 1, pair, back_even, zero)
-            put(even, pair - 1, zero, k_even)
-
-    for t in range(TILES):
-        lo, hi = reach(t)
-        mine = slice(t * TILE, (t + 1) * TILE)
-        near = slice(lo - base(t), hi - base(t))
-        if transposed:
-            one = dense[lo:hi, mine]
+    for block, t_ref, e_ref in ((x_block, xt_ref, xe_ref), (y_block, yt_ref, ye_ref)):
+        for pair in range(BLOCKS // 2):
+            even, odd = 2 * pair, 2 * pair + 1
+            d_even, k_even, back_even = split(block(even))
+            d_odd, k_odd, back_odd = split(block(odd))
+            put(even, pair, d_even, back_odd)
+            put(odd, pair, k_odd, d_odd)
+            if pair > 0:
+                put(even - 1, pair, back_even, zero)
+                put(even, pair - 1, zero, k_even)
+        for t in range(TILES):
+            lo, hi = reach(t)
+            near = slice(lo - base(t), hi - base(t))
+            one = dense[lo:hi, t * TILE : (t + 1) * TILE]
             two = jnp.dot(dense[lo:hi, lo:hi], one, preferred_element_type=F32)
-        else:
-            one = dense[mine, lo:hi]
-            two = jnp.dot(one, dense[lo:hi, lo:hi], preferred_element_type=F32)
-        two = ((2.0 * NUGGET) * one.astype(F32) + two).astype(BF16)
-        if transposed:
             t_ref[t, near, :] = one
-            e_ref[t, near, :] = two
-        else:
-            t_ref[t, :, near] = one
-            e_ref[t, :, near] = two
-
-
-def bands(place, mine, theirs, transposed):
-    shape = (TILES, 2 * TILE, TILE) if transposed else (TILES, TILE, 2 * TILE)
+            e_ref[t, near, :] = ((2.0 * NUGGET) * one.astype(F32) + two).astype(BF16)
+
+
+def bands(place, xmats, mine, theirs):
     vmem = pl.BlockSpec(memory_space=VMEM)
     return pl.pallas_call(
-        functools.partial(band_kernel, transposed),
-        out_shape=(jax.ShapeDtypeStruct(shape, BF16),) * 2,
-        in_specs=[pl.BlockSpec(memory_space=SMEM), vmem, vmem],
-        out_specs=(vmem, vmem),
+        band_kernel,
+        out_shape=(jax.ShapeDtypeStruct((TILES, 2 * TILE, TILE), BF16),) * 4,
+        in_specs=[pl.BlockSpec(memory_space=SMEM), vmem, vmem, vmem],
+        out_specs=(vmem,) * 4,
         scratch_shapes=[VMEM((N, N), BF16)],
-        compiler_params=pltpu.CompilerParams(vmem_limit_bytes=12 * 1024 * 1024),
+        compiler_params=pltpu.CompilerParams(vmem_limit_bytes=16 * 1024 * 1024),
         cost_estimate=pl.CostEstimate(
-            flops=2 * 4 * TILE * TILE * 4 * TILE, bytes_accessed=3 * 1024 * 1024, transcendentals=0
+            flops=4 * 4 * TILE * TILE * 4 * TILE, bytes_accessed=6 * 1024 * 1024, transcendentals=0
         ),
-        name="x_bands" if transposed else "y_bands",
-    )(place, mine, theirs)
+        name="bands",
+    )(place, xmats, mine, theirs)
 
 
 def sample_kernel(
@@ -248,12 +240,21 @@
             ub[:, cols] = value.astype(BF16)
 
     def along_y(band, share, finish):
-        for t in range(TILES):
-            lo, hi = reach(t)
-            rows = slice(t * TILE, (t + 1) * TILE)
-            matrix = band[t, :, lo - base(t) : hi - base(t)]
-            part = jnp.dot(matrix, ub[lo:hi, :], preferred_element_type=F32)
-            finish(rows, share * uf[rows, :] + part)
+        for k in range(TILES):
+            lo, hi = reach(k)
+            matrix = band[k, lo - base(k) : hi - base(k), :]
+            part = jnp.dot(matrix, ub[k * TILE : (k + 1) * TILE, :], preferred_element_type=F32)
+            for j in range(lo // S, hi // S):
+                rows = slice(j * S, (j + 1) * S)
+                value = part[j * S - lo : (j + 1) * S - lo]
+                if k == max(0, (j - 1) // 2):
+                    value = share * uf[rows, :] + value
+                else:
+                    value = uf[rows, :] + value
+                if k == min(TILES - 1, (j + 1) // 2):
+                    finish(rows, value)
+                else:
+                    uf[rows, :] = value
 
     c = [coeff_ref[i] for i in range(6)]
     square = NUGGET * NUGGET
@@ -363,26 +364,28 @@
         weights,
         track_obs,
     )
-    xfar = gather_ring(xpay, "zh")
+    turned = [((zh + v) % 4 * 4 + v, zh * 4 + v) for zh in range(4) for v in range(4)]
+    xfar = lax.ppermute(xpay, ("zh", "y"), turned)
     yfar = gather_ring(ypay, "zl")
     sent = split_samples(noise)
     sent, xfar, yfar = lax.optimization_barrier((sent, xfar, yfar))
     own = lax.all_to_all(sent, chips, 0, 0, tiled=True)
 
+    yfar = yfar.at[:, 16 : 16 + HALF, 3 * S : 4 * S].set(xfar.reshape(2, HALF, S))
+    ymine = gather_ring(yfar, "y").reshape(8, BLK, 4 * S)
+    xfar = ymine[:, 16 : 16 + HALF, 3 * S : 4 * S].reshape(4, BLK, S)
     xmats = gather_ring(xfar, "x").reshape(16, BLK, S)
-    ymine = gather_ring(yfar, "y").reshape(8, BLK, 4 * S)
     ytheirs = lax.ppermute(ymine, "core", [(0, 1), (1, 0)])
     own, xmats, ymine, ytheirs = lax.optimization_barrier((own, xmats, ymine, ytheirs))
     other = lax.ppermute(own, "core", [(0, 1), (1, 0)])
 
     index = jnp.arange(16, dtype=jnp.int32)
     near = (lax.axis_index("x") - index % 4) % 4
-    far = (lax.axis_index("zh") - index // 4) % 4
-    xt, xe = bands(near * 4 + far, xmats, xmats[0:1], True)
-    index = jnp.arange(9, dtype=jnp.int32)
-    place = (y - index // 2) % 4 * 2 + (zl - index) % 2
-    place = jnp.where(index == 8, core, place).astype(jnp.int32)
-    yt, ye = bands(place, ymine, ytheirs, False)
+    far = (y + lax.axis_index("zh") - index // 4) % 4
+    spot = (y - index // 2) % 4 * 2 + (zl - index) % 2
+    spot = jnp.where(index == 8, core, spot)
+    place = jnp.concatenate([spot, near * 4 + far]).astype(jnp.int32)
+    xt, xe, yt, ye = bands(place, xmats, ymine, ytheirs)
     extras = jnp.stack([ymine, ytheirs])[:, :, 0:16, 3 * S : 4 * S]
     rows = extras[:, :, 8:16, BLK].astype(jnp.int32).reshape(S)
 

time: 117 us -> 116 us (level)
  local copies, waits for them, and re-layouts: 1.66 us -> 0.45 us
    ppermute x10 -> x7, starting transfers between devices: 18.2 us -> 9.71 us  [gather_ring(): lax.ppermute(value, axis, [(i, (i + step) % size) for i in range(size)])]
    all_to_all x1, starting transfers between devices: 11.9 us -> 19.3 us  [body(): own = lax.all_to_all(sent, chips, 0, 0, tiled=True)]
    ppermute x0 -> x1, starting transfers between devices: none -> 1.36 us  [body(): xfar = lax.ppermute(xpay, ('zh', 'y'), turned)]
    unnamed x10 -> x6, local copies, waits for them, and re-layouts: 1.24 us -> 0.01 us
    pallas_call x2 -> x1, Pallas kernels: 3.09 us -> 2.29 us  [bands(): pl.pallas_call(band_kernel, out_shape=(jax.ShapeDtypeStruct((TILES, 2 * T...]
    ppermute x10 -> x7, waiting for transfers between devices: 19.5 us -> 19.2 us  [gather_ring(): lax.ppermute(value, axis, [(i, (i + step) % size) for i in range(size)])]
  transfers between devices with their start and end apart: 14 -> 12, of which waited for: 8 -> 8; matrix products, arithmetic and copies ran while one was open for 1% -> 1% of each run, Pallas kernels for 4% -> 4%
where the time goes in v4:
time: 116 us
  waiting for transfers between devices  49.6 us (43%)
  starting transfers between devices  42.5 us (37%)
  Pallas kernels  22.1 us (19%)
    all_to_all x1, waiting for transfers between devices, body(): back = lax.all_to_all(result.reshape(S, HALF, S), chips, 0, 0, tiled=True)  29.9 us
    all_to_all x1, starting transfers between devices, body(): own = lax.all_to_all(sent, chips, 0, 0, tiled=True)  19.3 us
    ppermute x7, waiting for transfers between devices, gather_ring(): lax.ppermute(value, axis, [(i, (i + step) % size) for i in range(size)])  19.2 us
    pallas_call x1, Pallas kernels, sample_all(): pl.pallas_call(sample_kernel, out_shape=jax.ShapeDtypeStruct((16, 8, HALF...  13.2 us
    ppermute x7, starting transfers between devices, gather_ring(): lax.ppermute(value, axis, [(i, (i + step) % size) for i in range(size)])  9.71 us
    all_to_all x1, starting transfers between devices, body(): back = lax.all_to_all(result.reshape(S, HALF, S), chips, 0, 0, tiled=True)  6.4 us
    ppermute x1, starting transfers between devices, body(): other = lax.ppermute(own, 'core', [(0, 1), (1, 0)])  4.16 us
    pallas_call x1, Pallas kernels, split_samples(): pl.pallas_call(split_samples_kernel, grid=(HALF // rows,), out_shape=jax....  2.64 us
  transfers between devices with their start and end apart: 12, of which 8 were waited for; matrix products, arithmetic and copies ran while one was open for 1% of the time, Pallas kernels for 4%

profile of v4, /device:TPU:1, one launch (start us, length us, event | category | flops | bytes accessed | tf_op | source)
XLA Modules:
  0.0 116.0 jit_solution(6693651955230821343)
XLA Ops:
  0.0 1.6 %payloads.1 = (bf16[64,128]{1,0:T(8,128)(2,1)}, bf16[64,512]{1,0:T(8,128)(2,1)}) custom-call(s32[1]{0:T(128)} %bitcast.1.block_ref, s32[8]{0:T(128)} %track_ref.1, f32[64,64]{1,0:T(8,128)} %dx_ref.1, bf16[64,64]{1,0:T(8,128)(2,1)} %kx_ref.1, f32[64,64]{1,0:T(8,128)} %dy_ref.1, bf16[64,64]{1,0:T(8,128)(2,1)} %ky_ref.1, f32[64,128]{1,0:T(8,128)} %weights_ref.1, ...), custom_call_target="tpu_custom_call" | custom-call | tf_op jit(solution)/shard_map/payloads/pallas_call | solution.py:118
  1.6 2.5 %collective-permute-start.1 = (bf16[64,512]{1,0:T(8,128)(2,1)}, bf16[64,512]{1,0:T(8,128)(2,1)S(1)}, u32[]{:S(2)}, u32[]{:S(2)}) collective-permute-start(bf16[64,512]{1,0:T(8,128)(2,1)} %get-tuple-element.31), channel_id=1, source_target_pairs={{0,2},{2,0},{1,3},{3,1},{4,6},{6,4},{5,7},{7,5},{8,10},{10,8},{9,1... | collective-permute-start | bytes 196616 | tf_op jit(solution)/shard_map/ppermute | solution.py:345
  4.0 1.4 %collective-permute-start = (bf16[64,128]{1,0:T(8,128)(2,1)}, bf16[64,128]{1,0:T(8,128)(2,1)S(1)}, u32[]{:S(2)}, u32[]{:S(2)}) collective-permute-start(bf16[64,128]{1,0:T(8,128)(2,1)} %get-tuple-element.30), channel_id=1, source_target_pairs={{0,0},{68,4},{136,8},{204,12},{64,64},{132,68},{200,72},{12,76},{1... | collective-permute-start | bytes 49160 | tf_op jit(solution)/shard_map/ppermute | solution.py:368
  5.4 2.6 %split_samples.1 = bf16[128,32,128]{2,1,0:T(8,128)(2,1)} custom-call(bf16[2,32,64,128]{3,2,1,0:T(8,128)(2,1)} %bitcast.44), custom_call_target="tpu_custom_call" | custom-call | bytes 2097152 | tf_op jit(solution)/shard_map/split_samples/pallas_call | solution.py:42
  8.1 19.3 %all-to-all-start = ((bf16[128,32,128]{2,1,0:T(8,128)(2,1)}), bf16[128,32,128]{2,1,0:T(8,128)(2,1)S(1)}, u32[]{:S(2)}, u32[]{:S(2)}) async-start(bf16[128,32,128]{2,1,0:T(8,128)(2,1)} %split_samples.1), calls=%async_computation | async-start | bytes 2097152 | tf_op jit(solution)/shard_map/all_to_all | solution.py:372
  27.4 1.9 %collective-permute-start.4 = (bf16[2,64,512]{2,1,0:T(8,128)(2,1)S(1)}, bf16[2,64,512]{2,1,0:T(8,128)(2,1)S(1)}, u32[]{:S(2)}, u32[]{:S(2)}) collective-permute-start(bf16[2,64,512]{2,1,0:T(8,128)(2,1)S(1)} %constant_dynamic-update-slice_fusion), channel_id=1, source_target_pairs={{0,12},{4,0},{8,4},{12,8},{1,13},{5,1},{9,5},{13,9},{2,14},{6,2},{... | collective-permute-start | bytes 393224 | tf_op jit(solution)/shard_map/ppermute | solution.py:345
  29.3 0.6 collective-permute-start.3
  29.9 0.6 collective-permute-start.2
  30.4 3.3 %collective-permute-done.4 = bf16[2,64,512]{2,1,0:T(8,128)(2,1)S(1)} collective-permute-done((bf16[2,64,512]{2,1,0:T(8,128)(2,1)S(1)}, bf16[2,64,512]{2,1,0:T(8,128)(2,1)S(1)}, u32[]{:S(2)}, u32[]{:S(2)}) %collective-permute-start.4) | collective-permute-done | bytes 131104 | tf_op jit(solution)/shard_map/ppermute | solution.py:345
  33.7 2.9 %collective-permute-done.3 = bf16[2,64,512]{2,1,0:T(8,128)(2,1)S(1)} collective-permute-done((bf16[2,64,512]{2,1,0:T(8,128)(2,1)S(1)}, bf16[2,64,512]{2,1,0:T(8,128)(2,1)S(1)}, u32[]{:S(2)}, u32[]{:S(2)}) %collective-permute-start.3) | collective-permute-done | bytes 131104 | tf_op jit(solution)/shard_map/ppermute | solution.py:345
  36.7 5.9 %collective-permute-done.2 = bf16[2,64,512]{2,1,0:T(8,128)(2,1)S(1)} collective-permute-done((bf16[2,64,512]{2,1,0:T(8,128)(2,1)S(1)}, bf16[2,64,512]{2,1,0:T(8,128)(2,1)S(1)}, u32[]{:S(2)}, u32[]{:S(2)}) %collective-permute-start.2) | collective-permute-done | bytes 131104 | tf_op jit(solution)/shard_map/ppermute | solution.py:345
  42.7 1.5 %collective-permute-start.8 = (bf16[8,64,512]{2,1,0:T(8,128)(2,1)S(1)}, bf16[8,64,512]{2,1,0:T(8,128)(2,1)S(1)}, u32[]{:S(2)}, u32[]{:S(2)}) collective-permute-start(bf16[8,64,512]{2,1,0:T(8,128)(2,1)S(1)} %bitcast.33), channel_id=1, source_target_pairs={{0,1},{1,0},{2,3},{3,2},{4,5},{5,4},{6,7},{7,6},{8,9},{9,8},{10,11... | collective-permute-start | bytes 1572872 | tf_op jit(solution)/shard_map/ppermute | solution.py:378
  44.2 3.2 %collective-permute-start.7 = (bf16[4,64,128]{2,1,0:T(8,128)(2,1)S(1)}, bf16[4,64,128]{2,1,0:T(8,128)(2,1)S(1)}, u32[]{:S(2)}, u32[]{:S(2)}) collective-permute-start(bf16[4,64,128]{2,1,0:T(8,128)(2,1)S(1)} %bitcast.46), channel_id=1, source_target_pairs={{0,48},{16,0},{32,16},{48,32},{1,49},{17,1},{33,17},{49,33},{2,50}... | collective-permute-start | bytes 196616 | tf_op jit(solution)/shard_map/ppermute | solution.py:345
  47.4 0.7 collective-permute-start.6
  48.5 1.6 %collective-permute-done.7 = bf16[4,64,128]{2,1,0:T(8,128)(2,1)S(1)} collective-permute-done((bf16[4,64,128]{2,1,0:T(8,128)(2,1)S(1)}, bf16[4,64,128]{2,1,0:T(8,128)(2,1)S(1)}, u32[]{:S(2)}, u32[]{:S(2)}) %collective-permute-start.7) | collective-permute-done | bytes 65568 | tf_op jit(solution)/shard_map/ppermute | solution.py:345
  50.1 3.7 %collective-permute-done.6 = bf16[4,64,128]{2,1,0:T(8,128)(2,1)S(1)} collective-permute-done((bf16[4,64,128]{2,1,0:T(8,128)(2,1)S(1)}, bf16[4,64,128]{2,1,0:T(8,128)(2,1)S(1)}, u32[]{:S(2)}, u32[]{:S(2)}) %collective-permute-start.6) | collective-permute-done | bytes 65568 | tf_op jit(solution)/shard_map/ppermute | solution.py:345
  53.8 1.6 %collective-permute-done.5 = bf16[4,64,128]{2,1,0:T(8,128)(2,1)S(1)} collective-permute-done((bf16[4,64,128]{2,1,0:T(8,128)(2,1)S(1)}, bf16[4,64,128]{2,1,0:T(8,128)(2,1)S(1)}, u32[]{:S(2)}, u32[]{:S(2)}) %collective-permute-start.5) | collective-permute-done | bytes 65568 | tf_op jit(solution)/shard_map/ppermute | solution.py:345
  55.5 0.5 all-to-all-done
  56.0 4.2 %collective-permute-start.9 = (bf16[128,32,128]{2,1,0:T(8,128)(2,1)S(1)}, bf16[128,32,128]{2,1,0:T(8,128)(2,1)S(1)}, u32[]{:S(2)}, u32[]{:S(2)}) collective-permute-start(bf16[128,32,128]{2,1,0:T(8,128)(2,1)S(1)} %all-to-all-done), channel_id=1, source_target_pairs={{0,1},{1,0},{2,3},{3,2},{4,5},{5,4},{6,7},{7,6},{8,9},{9,8},{10,11... | collective-permute-start | bytes 3145736 | tf_op jit(solution)/shard_map/ppermute | solution.py:380
  60.7 2.3 %bands.1 = (bf16[4,512,256]{2,1,0:T(8,128)(2,1)S(1)}, bf16[4,512,256]{2,1,0:T(8,128)(2,1)S(1)}, bf16[4,512,256]{2,1,0:T(8,128)(2,1)S(1)}, bf16[4,512,256]{2,1,0:T(8,128)(2,1)S(1)}) custom-call(s32[32]{0:T(128)S(1)} %pad_add_fusion.place_ref, bf16[16,64,128]{2,1,0:T(8,128)(2,1)S(1)} %bitcast.42, bf16[8,64,512]{2,1,0:T(8,128)(2,1)S(1)} %bitcast.36, ...), custom_call_target="tpu_custom_call" | custom-call | flops 1073741824 | bytes 6291456 | tf_op jit(solution)/shard_map/bands/pallas_call | solution.py:182
  63.1 13.2 %sample_all.1 = bf16[16,8,32,128]{3,2,1,0:T(8,128)(2,1)} custom-call(s32[32]{0:T(128)S(1)} %pad_add_fusion.place_ref, f32[6]{0:T(128)S(1)} %copy-done, s32[128]{0:T(128)S(1)} %reshape.157.rows_ref, bf16[16,8,32,128]{3,2,1,0:T(8,128)(2,1)S(1)} %bitcast.41, bf16[16,8,32,128]{3,2,1,0:T(8,128)(2,1)S(1)} %bitcast.43, ...), custom_call_target="tpu_custom_call" | custom-call | flops 6442450944 | bytes 5242880 | tf_op jit(solution)/shard_map/sample_all/pallas_call | solution.py:318
  76.2 6.4 %all-to-all-start.1 = ((bf16[128,32,128]{2,1,0:T(8,128)(2,1)}), bf16[128,32,128]{2,1,0:T(8,128)(2,1)S(1)}, u32[]{:S(2)}, u32[]{:S(2)}) async-start(bf16[128,32,128]{2,1,0:T(8,128)(2,1)} %bitcast.20), calls=%async_computation.1 | async-start | bytes 2097152 | tf_op jit(solution)/shard_map/all_to_all | solution.py:405
  83.6 29.9 %all-to-all-done.1.msg_ref = bf16[128,32,128]{2,1,0:T(8,128)(2,1)S(1)} async-done(((bf16[128,32,128]{2,1,0:T(8,128)(2,1)}), bf16[128,32,128]{2,1,0:T(8,128)(2,1)S(1)}, u32[]{:S(2)}, u32[]{:S(2)}) %all-to-all-start.1) | async-done | bytes 1048608 | tf_op jit(solution)/shard_map/all_to_all | solution.py:405
  113.5 2.4 %join_samples.1 = f32[2,32,64,128]{3,2,1,0:T(8,128)} custom-call(bf16[128,32,128]{2,1,0:T(8,128)(2,1)S(1)} %all-to-all-done.1.msg_ref, f32[2,64,32]{2,1,0:T(8,128)S(1)} %copy.13.extra_ref), custom_call_target="tpu_custom_call" | custom-call | bytes 3145728 | tf_op jit(solution)/shard_map/join_samples/pallas_call | solution.py:70
  (30 shorter events, 2.1 us)
Async XLA Ops:
  1.6 6.5 %copy-start.2 = (bf16[64,512]{1,0:T(8,128)(2,1)S(1)}, bf16[64,512]{1,0:T(8,128)(2,1)}, u32[]{:S(2)}) copy-start(bf16[64,512]{1,0:T(8,128)(2,1)} %get-tuple-element.31) | copy-start | bytes 196612
  1.6 6.5 %collective-permute-start.1 = (bf16[64,512]{1,0:T(8,128)(2,1)}, bf16[64,512]{1,0:T(8,128)(2,1)S(1)}, u32[]{:S(2)}, u32[]{:S(2)}) collective-permute-start(bf16[64,512]{1,0:T(8,128)(2,1)} %get-tuple-element.31), channel_id=1, source_target_pairs={{0,2},{2,0},{1,3},{3,1},{4,6},{6,4},{5,7},{7,5},{8,10},{10,8},{9,1... | collective-permute-start | bytes 196616 | tf_op jit(solution)/shard_map/ppermute | solution.py:345
  4.0 4.0 %collective-permute-start = (bf16[64,128]{1,0:T(8,128)(2,1)}, bf16[64,128]{1,0:T(8,128)(2,1)S(1)}, u32[]{:S(2)}, u32[]{:S(2)}) collective-permute-start(bf16[64,128]{1,0:T(8,128)(2,1)} %get-tuple-element.30), channel_id=1, source_target_pairs={{0,0},{68,4},{136,8},{204,12},{64,64},{132,68},{200,72},{12,76},{1... | collective-permute-start | bytes 49160 | tf_op jit(solution)/shard_map/ppermute | solution.py:368
  8.1 47.9 %all-to-all-start = ((bf16[128,32,128]{2,1,0:T(8,128)(2,1)}), bf16[128,32,128]{2,1,0:T(8,128)(2,1)S(1)}, u32[]{:S(2)}, u32[]{:S(2)}) async-start(bf16[128,32,128]{2,1,0:T(8,128)(2,1)} %split_samples.1), calls=%async_computation | async-start | bytes 2097152 | tf_op jit(solution)/shard_map/all_to_all | solution.py:372
  27.4 6.3 %collective-permute-start.4 = (bf16[2,64,512]{2,1,0:T(8,128)(2,1)S(1)}, bf16[2,64,512]{2,1,0:T(8,128)(2,1)S(1)}, u32[]{:S(2)}, u32[]{:S(2)}) collective-permute-start(bf16[2,64,512]{2,1,0:T(8,128)(2,1)S(1)} %constant_dynamic-update-slice_fusion), channel_id=1, source_target_pairs={{0,12},{4,0},{8,4},{12,8},{1,13},{5,1},{9,5},{13,9},{2,14},{6,2},{... | collective-permute-start | bytes 393224 | tf_op jit(solution)/shard_map/ppermute | solution.py:345
  29.3 7.4 %collective-permute-start.3 = (bf16[2,64,512]{2,1,0:T(8,128)(2,1)S(1)}, bf16[2,64,512]{2,1,0:T(8,128)(2,1)S(1)}, u32[]{:S(2)}, u32[]{:S(2)}) collective-permute-start(bf16[2,64,512]{2,1,0:T(8,128)(2,1)S(1)} %constant_dynamic-update-slice_fusion), channel_id=1, source_target_pairs={{0,8},{4,12},{8,0},{12,4},{1,9},{5,13},{9,1},{13,5},{2,10},{6,14},... | collective-permute-start | bytes 393224 | tf_op jit(solution)/shard_map/ppermute | solution.py:345
  29.9 12.8 %collective-permute-start.2 = (bf16[2,64,512]{2,1,0:T(8,128)(2,1)S(1)}, bf16[2,64,512]{2,1,0:T(8,128)(2,1)S(1)}, u32[]{:S(2)}, u32[]{:S(2)}) collective-permute-start(bf16[2,64,512]{2,1,0:T(8,128)(2,1)S(1)} %constant_dynamic-update-slice_fusion), channel_id=1, source_target_pairs={{0,4},{4,8},{8,12},{12,0},{1,5},{5,9},{9,13},{13,1},{2,6},{6,10},{... | collective-permute-start | bytes 393224 | tf_op jit(solution)/shard_map/ppermute | solution.py:345
  42.7 12.8 %collective-permute-start.8 = (bf16[8,64,512]{2,1,0:T(8,128)(2,1)S(1)}, bf16[8,64,512]{2,1,0:T(8,128)(2,1)S(1)}, u32[]{:S(2)}, u32[]{:S(2)}) collective-permute-start(bf16[8,64,512]{2,1,0:T(8,128)(2,1)S(1)} %bitcast.33), channel_id=1, source_target_pairs={{0,1},{1,0},{2,3},{3,2},{4,5},{5,4},{6,7},{7,6},{8,9},{9,8},{10,11... | collective-permute-start | bytes 1572872 | tf_op jit(solution)/shard_map/ppermute | solution.py:378
  44.2 5.8 %collective-permute-start.7 = (bf16[4,64,128]{2,1,0:T(8,128)(2,1)S(1)}, bf16[4,64,128]{2,1,0:T(8,128)(2,1)S(1)}, u32[]{:S(2)}, u32[]{:S(2)}) collective-permute-start(bf16[4,64,128]{2,1,0:T(8,128)(2,1)S(1)} %bitcast.46), channel_id=1, source_target_pairs={{0,48},{16,0},{32,16},{48,32},{1,49},{17,1},{33,17},{49,33},{2,50}... | collective-permute-start | bytes 196616 | tf_op jit(solution)/shard_map/ppermute | solution.py:345
  47.4 6.4 %collective-permute-start.6 = (bf16[4,64,128]{2,1,0:T(8,128)(2,1)S(1)}, bf16[4,64,128]{2,1,0:T(8,128)(2,1)S(1)}, u32[]{:S(2)}, u32[]{:S(2)}) collective-permute-start(bf16[4,64,128]{2,1,0:T(8,128)(2,1)S(1)} %bitcast.47), channel_id=1, source_target_pairs={{0,32},{16,48},{32,0},{48,16},{1,33},{17,49},{33,1},{49,17},{2,34}... | collective-permute-start | bytes 196616 | tf_op jit(solution)/shard_map/ppermute | solution.py:345
  48.0 7.4 %collective-permute-start.5 = (bf16[4,64,128]{2,1,0:T(8,128)(2,1)S(1)}, bf16[4,64,128]{2,1,0:T(8,128)(2,1)S(1)}, u32[]{:S(2)}, u32[]{:S(2)}) collective-permute-start(bf16[4,64,128]{2,1,0:T(8,128)(2,1)S(1)} %bitcast.48), channel_id=1, source_target_pairs={{0,16},{16,32},{32,48},{48,0},{1,17},{17,33},{33,49},{49,1},{2,18}... | collective-permute-start | bytes 196616 | tf_op jit(solution)/shard_map/ppermute | solution.py:345
  56.0 7.1 %collective-permute-start.9 = (bf16[128,32,128]{2,1,0:T(8,128)(2,1)S(1)}, bf16[128,32,128]{2,1,0:T(8,128)(2,1)S(1)}, u32[]{:S(2)}, u32[]{:S(2)}) collective-permute-start(bf16[128,32,128]{2,1,0:T(8,128)(2,1)S(1)} %all-to-all-done), channel_id=1, source_target_pairs={{0,1},{1,0},{2,3},{3,2},{4,5},{5,4},{6,7},{7,6},{8,9},{9,8},{10,11... | collective-permute-start | bytes 3145736 | tf_op jit(solution)/shard_map/ppermute | solution.py:380
  60.6 2.4 %copy-start = (f32[6]{0:T(128)S(1)}, f32[6]{0:T(128)}, u32[]{:S(2)}) copy-start(f32[6]{0:T(128)} %coeff_ref.1) | copy-start | bytes 76
  76.2 6.9 %copy-start.1 = (f32[64,128]{1,0:T(8,128)S(1)}, f32[64,128]{1,0:T(8,128)}, u32[]{:S(2)}) copy-start(f32[64,128]{1,0:T(8,128)} %weights_ref.1) | copy-start | bytes 98308
  76.2 37.3 %all-to-all-start.1 = ((bf16[128,32,128]{2,1,0:T(8,128)(2,1)}), bf16[128,32,128]{2,1,0:T(8,128)(2,1)S(1)}, u32[]{:S(2)}, u32[]{:S(2)}) async-start(bf16[128,32,128]{2,1,0:T(8,128)(2,1)} %bitcast.20), calls=%async_computation.1 | async-start | bytes 2097152 | tf_op jit(solution)/shard_map/all_to_all | solution.py:405

commit v5 on v4

--- a/solution.py
+++ b/solution.py
@@ -38,7 +38,7 @@
 
 
 def split_samples(noise):
-    rows = 16
+    rows = 8
     return pl.pallas_call(
         split_samples_kernel,
         grid=(HALF // rows,),

time: 116 us -> 116 us (level)
  transfers between devices with their start and end apart: 12 -> 12, of which waited for: 8 -> 8; matrix products, arithmetic and copies ran while one was open for 1% -> 1% of each run, Pallas kernels for 4% -> 5%
where the time goes in v5:
time: 116 us
  waiting for transfers between devices  49.6 us (43%)
  starting transfers between devices  41.5 us (36%)
  Pallas kernels  23.1 us (20%)
    all_to_all x1, waiting for transfers between devices, body(): back = lax.all_to_all(result.reshape(S, HALF, S), chips, 0, 0, tiled=True)  29.9 us
    ppermute x7, waiting for transfers between devices, gather_ring(): lax.ppermute(value, axis, [(i, (i + step) % size) for i in range(size)])  19.2 us
    all_to_all x1, starting transfers between devices, body(): own = lax.all_to_all(sent, chips, 0, 0, tiled=True)  18.3 us
    pallas_call x1, Pallas kernels, sample_all(): pl.pallas_call(sample_kernel, out_shape=jax.ShapeDtypeStruct((16, 8, HALF...  13.2 us
    ppermute x7, starting transfers between devices, gather_ring(): lax.ppermute(value, axis, [(i, (i + step) % size) for i in range(size)])  9.71 us
    all_to_all x1, starting transfers between devices, body(): back = lax.all_to_all(result.reshape(S, HALF, S), chips, 0, 0, tiled=True)  6.4 us
    ppermute x1, starting transfers between devices, body(): other = lax.ppermute(own, 'core', [(0, 1), (1, 0)])  4.16 us
    pallas_call x1, Pallas kernels, split_samples(): pl.pallas_call(split_samples_kernel, grid=(HALF // rows,), out_shape=jax....  3.65 us
  transfers between devices with their start and end apart: 12, of which 8 were waited for; matrix products, arithmetic and copies ran while one was open for 1% of the time, Pallas kernels for 5%

profile of v5, /device:TPU:1, one launch (start us, length us, event | category | flops | bytes accessed | tf_op | source)
XLA Modules:
  0.0 116.0 jit_solution(4889015173628380298)
XLA Ops:
  0.0 1.6 %payloads.1 = (bf16[64,128]{1,0:T(8,128)(2,1)}, bf16[64,512]{1,0:T(8,128)(2,1)}) custom-call(s32[1]{0:T(128)} %bitcast.1.block_ref, s32[8]{0:T(128)} %track_ref.1, f32[64,64]{1,0:T(8,128)} %dx_ref.1, bf16[64,64]{1,0:T(8,128)(2,1)} %kx_ref.1, f32[64,64]{1,0:T(8,128)} %dy_ref.1, bf16[64,64]{1,0:T(8,128)(2,1)} %ky_ref.1, f32[64,128]{1,0:T(8,128)} %weights_ref.1, ...), custom_call_target="tpu_custom_call" | custom-call | tf_op jit(solution)/shard_map/payloads/pallas_call | solution.py:118
  1.6 2.5 %collective-permute-start.1 = (bf16[64,512]{1,0:T(8,128)(2,1)}, bf16[64,512]{1,0:T(8,128)(2,1)S(1)}, u32[]{:S(2)}, u32[]{:S(2)}) collective-permute-start(bf16[64,512]{1,0:T(8,128)(2,1)} %get-tuple-element.31), channel_id=1, source_target_pairs={{0,2},{2,0},{1,3},{3,1},{4,6},{6,4},{5,7},{7,5},{8,10},{10,8},{9,1... | collective-permute-start | bytes 196616 | tf_op jit(solution)/shard_map/ppermute | solution.py:345
  4.0 1.4 %collective-permute-start = (bf16[64,128]{1,0:T(8,128)(2,1)}, bf16[64,128]{1,0:T(8,128)(2,1)S(1)}, u32[]{:S(2)}, u32[]{:S(2)}) collective-permute-start(bf16[64,128]{1,0:T(8,128)(2,1)} %get-tuple-element.30), channel_id=1, source_target_pairs={{0,0},{68,4},{136,8},{204,12},{64,64},{132,68},{200,72},{12,76},{1... | collective-permute-start | bytes 49160 | tf_op jit(solution)/shard_map/ppermute | solution.py:368
  5.4 3.7 %split_samples.1 = bf16[128,32,128]{2,1,0:T(8,128)(2,1)} custom-call(bf16[2,32,64,128]{3,2,1,0:T(8,128)(2,1)} %bitcast.44), custom_call_target="tpu_custom_call" | custom-call | bytes 2097152 | tf_op jit(solution)/shard_map/split_samples/pallas_call | solution.py:42
  9.1 18.3 %all-to-all-start = ((bf16[128,32,128]{2,1,0:T(8,128)(2,1)}), bf16[128,32,128]{2,1,0:T(8,128)(2,1)S(1)}, u32[]{:S(2)}, u32[]{:S(2)}) async-start(bf16[128,32,128]{2,1,0:T(8,128)(2,1)} %split_samples.1), calls=%async_computation | async-start | bytes 2097152 | tf_op jit(solution)/shard_map/all_to_all | solution.py:372
  27.4 1.9 %collective-permute-start.4 = (bf16[2,64,512]{2,1,0:T(8,128)(2,1)S(1)}, bf16[2,64,512]{2,1,0:T(8,128)(2,1)S(1)}, u32[]{:S(2)}, u32[]{:S(2)}) collective-permute-start(bf16[2,64,512]{2,1,0:T(8,128)(2,1)S(1)} %constant_dynamic-update-slice_fusion), channel_id=1, source_target_pairs={{0,12},{4,0},{8,4},{12,8},{1,13},{5,1},{9,5},{13,9},{2,14},{6,2},{... | collective-permute-start | bytes 393224 | tf_op jit(solution)/shard_map/ppermute | solution.py:345
  29.3 0.6 collective-permute-start.3
  29.9 0.6 collective-permute-start.2
  30.4 3.3 %collective-permute-done.4 = bf16[2,64,512]{2,1,0:T(8,128)(2,1)S(1)} collective-permute-done((bf16[2,64,512]{2,1,0:T(8,128)(2,1)S(1)}, bf16[2,64,512]{2,1,0:T(8,128)(2,1)S(1)}, u32[]{:S(2)}, u32[]{:S(2)}) %collective-permute-start.4) | collective-permute-done | bytes 131104 | tf_op jit(solution)/shard_map/ppermute | solution.py:345
  33.7 2.9 %collective-permute-done.3 = bf16[2,64,512]{2,1,0:T(8,128)(2,1)S(1)} collective-permute-done((bf16[2,64,512]{2,1,0:T(8,128)(2,1)S(1)}, bf16[2,64,512]{2,1,0:T(8,128)(2,1)S(1)}, u32[]{:S(2)}, u32[]{:S(2)}) %collective-permute-start.3) | collective-permute-done | bytes 131104 | tf_op jit(solution)/shard_map/ppermute | solution.py:345
  36.7 5.9 %collective-permute-done.2 = bf16[2,64,512]{2,1,0:T(8,128)(2,1)S(1)} collective-permute-done((bf16[2,64,512]{2,1,0:T(8,128)(2,1)S(1)}, bf16[2,64,512]{2,1,0:T(8,128)(2,1)S(1)}, u32[]{:S(2)}, u32[]{:S(2)}) %collective-permute-start.2) | collective-permute-done | bytes 131104 | tf_op jit(solution)/shard_map/ppermute | solution.py:345
  42.7 1.5 %collective-permute-start.8 = (bf16[8,64,512]{2,1,0:T(8,128)(2,1)S(1)}, bf16[8,64,512]{2,1,0:T(8,128)(2,1)S(1)}, u32[]{:S(2)}, u32[]{:S(2)}) collective-permute-start(bf16[8,64,512]{2,1,0:T(8,128)(2,1)S(1)} %bitcast.33), channel_id=1, source_target_pairs={{0,1},{1,0},{2,3},{3,2},{4,5},{5,4},{6,7},{7,6},{8,9},{9,8},{10,11... | collective-permute-start | bytes 1572872 | tf_op jit(solution)/shard_map/ppermute | solution.py:378
  44.2 3.2 %collective-permute-start.7 = (bf16[4,64,128]{2,1,0:T(8,128)(2,1)S(1)}, bf16[4,64,128]{2,1,0:T(8,128)(2,1)S(1)}, u32[]{:S(2)}, u32[]{:S(2)}) collective-permute-start(bf16[4,64,128]{2,1,0:T(8,128)(2,1)S(1)} %bitcast.46), channel_id=1, source_target_pairs={{0,48},{16,0},{32,16},{48,32},{1,49},{17,1},{33,17},{49,33},{2,50}... | collective-permute-start | bytes 196616 | tf_op jit(solution)/shard_map/ppermute | solution.py:345
  47.4 0.7 collective-permute-start.6
  48.5 1.6 %collective-permute-done.7 = bf16[4,64,128]{2,1,0:T(8,128)(2,1)S(1)} collective-permute-done((bf16[4,64,128]{2,1,0:T(8,128)(2,1)S(1)}, bf16[4,64,128]{2,1,0:T(8,128)(2,1)S(1)}, u32[]{:S(2)}, u32[]{:S(2)}) %collective-permute-start.7) | collective-permute-done | bytes 65568 | tf_op jit(solution)/shard_map/ppermute | solution.py:345
  50.1 3.7 %collective-permute-done.6 = bf16[4,64,128]{2,1,0:T(8,128)(2,1)S(1)} collective-permute-done((bf16[4,64,128]{2,1,0:T(8,128)(2,1)S(1)}, bf16[4,64,128]{2,1,0:T(8,128)(2,1)S(1)}, u32[]{:S(2)}, u32[]{:S(2)}) %collective-permute-start.6) | collective-permute-done | bytes 65568 | tf_op jit(solution)/shard_map/ppermute | solution.py:345
  53.8 1.6 %collective-permute-done.5 = bf16[4,64,128]{2,1,0:T(8,128)(2,1)S(1)} collective-permute-done((bf16[4,64,128]{2,1,0:T(8,128)(2,1)S(1)}, bf16[4,64,128]{2,1,0:T(8,128)(2,1)S(1)}, u32[]{:S(2)}, u32[]{:S(2)}) %collective-permute-start.5) | collective-permute-done | bytes 65568 | tf_op jit(solution)/shard_map/ppermute | solution.py:345
  55.5 0.5 all-to-all-done
  56.0 4.2 %collective-permute-start.9 = (bf16[128,32,128]{2,1,0:T(8,128)(2,1)S(1)}, bf16[128,32,128]{2,1,0:T(8,128)(2,1)S(1)}, u32[]{:S(2)}, u32[]{:S(2)}) collective-permute-start(bf16[128,32,128]{2,1,0:T(8,128)(2,1)S(1)} %all-to-all-done), channel_id=1, source_target_pairs={{0,1},{1,0},{2,3},{3,2},{4,5},{5,4},{6,7},{7,6},{8,9},{9,8},{10,11... | collective-permute-start | bytes 3145736 | tf_op jit(solution)/shard_map/ppermute | solution.py:380
  60.7 2.3 %bands.1 = (bf16[4,512,256]{2,1,0:T(8,128)(2,1)S(1)}, bf16[4,512,256]{2,1,0:T(8,128)(2,1)S(1)}, bf16[4,512,256]{2,1,0:T(8,128)(2,1)S(1)}, bf16[4,512,256]{2,1,0:T(8,128)(2,1)S(1)}) custom-call(s32[32]{0:T(128)S(1)} %pad_add_fusion.place_ref, bf16[16,64,128]{2,1,0:T(8,128)(2,1)S(1)} %bitcast.42, bf16[8,64,512]{2,1,0:T(8,128)(2,1)S(1)} %bitcast.36, ...), custom_call_target="tpu_custom_call" | custom-call | flops 1073741824 | bytes 6291456 | tf_op jit(solution)/shard_map/bands/pallas_call | solution.py:182
  63.1 13.2 %sample_all.1 = bf16[16,8,32,128]{3,2,1,0:T(8,128)(2,1)} custom-call(s32[32]{0:T(128)S(1)} %pad_add_fusion.place_ref, f32[6]{0:T(128)S(1)} %copy-done, s32[128]{0:T(128)S(1)} %reshape.157.rows_ref, bf16[16,8,32,128]{3,2,1,0:T(8,128)(2,1)S(1)} %bitcast.41, bf16[16,8,32,128]{3,2,1,0:T(8,128)(2,1)S(1)} %bitcast.43, ...), custom_call_target="tpu_custom_call" | custom-call | flops 6442450944 | bytes 5242880 | tf_op jit(solution)/shard_map/sample_all/pallas_call | solution.py:318
  76.2 6.4 %all-to-all-start.1 = ((bf16[128,32,128]{2,1,0:T(8,128)(2,1)}), bf16[128,32,128]{2,1,0:T(8,128)(2,1)S(1)}, u32[]{:S(2)}, u32[]{:S(2)}) async-start(bf16[128,32,128]{2,1,0:T(8,128)(2,1)} %bitcast.20), calls=%async_computation.1 | async-start | bytes 2097152 | tf_op jit(solution)/shard_map/all_to_all | solution.py:405
  83.6 29.9 %all-to-all-done.1.msg_ref = bf16[128,32,128]{2,1,0:T(8,128)(2,1)S(1)} async-done(((bf16[128,32,128]{2,1,0:T(8,128)(2,1)}), bf16[128,32,128]{2,1,0:T(8,128)(2,1)S(1)}, u32[]{:S(2)}, u32[]{:S(2)}) %all-to-all-start.1) | async-done | bytes 1048608 | tf_op jit(solution)/shard_map/all_to_all | solution.py:405
  113.5 2.4 %join_samples.1 = f32[2,32,64,128]{3,2,1,0:T(8,128)} custom-call(bf16[128,32,128]{2,1,0:T(8,128)(2,1)S(1)} %all-to-all-done.1.msg_ref, f32[2,64,32]{2,1,0:T(8,128)S(1)} %copy.13.extra_ref), custom_call_target="tpu_custom_call" | custom-call | bytes 3145728 | tf_op jit(solution)/shard_map/join_samples/pallas_call | solution.py:70
  (30 shorter events, 2.1 us)
Async XLA Ops:
  1.6 7.5 %copy-start.2 = (bf16[64,512]{1,0:T(8,128)(2,1)S(1)}, bf16[64,512]{1,0:T(8,128)(2,1)}, u32[]{:S(2)}) copy-start(bf16[64,512]{1,0:T(8,128)(2,1)} %get-tuple-element.31) | copy-start | bytes 196612
  1.6 7.5 %collective-permute-start.1 = (bf16[64,512]{1,0:T(8,128)(2,1)}, bf16[64,512]{1,0:T(8,128)(2,1)S(1)}, u32[]{:S(2)}, u32[]{:S(2)}) collective-permute-start(bf16[64,512]{1,0:T(8,128)(2,1)} %get-tuple-element.31), channel_id=1, source_target_pairs={{0,2},{2,0},{1,3},{3,1},{4,6},{6,4},{5,7},{7,5},{8,10},{10,8},{9,1... | collective-permute-start | bytes 196616 | tf_op jit(solution)/shard_map/ppermute | solution.py:345
  4.0 5.0 %collective-permute-start = (bf16[64,128]{1,0:T(8,128)(2,1)}, bf16[64,128]{1,0:T(8,128)(2,1)S(1)}, u32[]{:S(2)}, u32[]{:S(2)}) collective-permute-start(bf16[64,128]{1,0:T(8,128)(2,1)} %get-tuple-element.30), channel_id=1, source_target_pairs={{0,0},{68,4},{136,8},{204,12},{64,64},{132,68},{200,72},{12,76},{1... | collective-permute-start | bytes 49160 | tf_op jit(solution)/shard_map/ppermute | solution.py:368
  9.1 46.9 %all-to-all-start = ((bf16[128,32,128]{2,1,0:T(8,128)(2,1)}), bf16[128,32,128]{2,1,0:T(8,128)(2,1)S(1)}, u32[]{:S(2)}, u32[]{:S(2)}) async-start(bf16[128,32,128]{2,1,0:T(8,128)(2,1)} %split_samples.1), calls=%async_computation | async-start | bytes 2097152 | tf_op jit(solution)/shard_map/all_to_all | solution.py:372
  27.4 6.3 %collective-permute-start.4 = (bf16[2,64,512]{2,1,0:T(8,128)(2,1)S(1)}, bf16[2,64,512]{2,1,0:T(8,128)(2,1)S(1)}, u32[]{:S(2)}, u32[]{:S(2)}) collective-permute-start(bf16[2,64,512]{2,1,0:T(8,128)(2,1)S(1)} %constant_dynamic-update-slice_fusion), channel_id=1, source_target_pairs={{0,12},{4,0},{8,4},{12,8},{1,13},{5,1},{9,5},{13,9},{2,14},{6,2},{... | collective-permute-start | bytes 393224 | tf_op jit(solution)/shard_map/ppermute | solution.py:345
  29.3 7.4 %collective-permute-start.3 = (bf16[2,64,512]{2,1,0:T(8,128)(2,1)S(1)}, bf16[2,64,512]{2,1,0:T(8,128)(2,1)S(1)}, u32[]{:S(2)}, u32[]{:S(2)}) collective-permute-start(bf16[2,64,512]{2,1,0:T(8,128)(2,1)S(1)} %constant_dynamic-update-slice_fusion), channel_id=1, source_target_pairs={{0,8},{4,12},{8,0},{12,4},{1,9},{5,13},{9,1},{13,5},{2,10},{6,14},... | collective-permute-start | bytes 393224 | tf_op jit(solution)/shard_map/ppermute | solution.py:345
  29.9 12.8 %collective-permute-start.2 = (bf16[2,64,512]{2,1,0:T(8,128)(2,1)S(1)}, bf16[2,64,512]{2,1,0:T(8,128)(2,1)S(1)}, u32[]{:S(2)}, u32[]{:S(2)}) collective-permute-start(bf16[2,64,512]{2,1,0:T(8,128)(2,1)S(1)} %constant_dynamic-update-slice_fusion), channel_id=1, source_target_pairs={{0,4},{4,8},{8,12},{12,0},{1,5},{5,9},{9,13},{13,1},{2,6},{6,10},{... | collective-permute-start | bytes 393224 | tf_op jit(solution)/shard_map/ppermute | solution.py:345
  42.7 12.8 %collective-permute-start.8 = (bf16[8,64,512]{2,1,0:T(8,128)(2,1)S(1)}, bf16[8,64,512]{2,1,0:T(8,128)(2,1)S(1)}, u32[]{:S(2)}, u32[]{:S(2)}) collective-permute-start(bf16[8,64,512]{2,1,0:T(8,128)(2,1)S(1)} %bitcast.33), channel_id=1, source_target_pairs={{0,1},{1,0},{2,3},{3,2},{4,5},{5,4},{6,7},{7,6},{8,9},{9,8},{10,11... | collective-permute-start | bytes 1572872 | tf_op jit(solution)/shard_map/ppermute | solution.py:378
  44.2 5.8 %collective-permute-start.7 = (bf16[4,64,128]{2,1,0:T(8,128)(2,1)S(1)}, bf16[4,64,128]{2,1,0:T(8,128)(2,1)S(1)}, u32[]{:S(2)}, u32[]{:S(2)}) collective-permute-start(bf16[4,64,128]{2,1,0:T(8,128)(2,1)S(1)} %bitcast.46), channel_id=1, source_target_pairs={{0,48},{16,0},{32,16},{48,32},{1,49},{17,1},{33,17},{49,33},{2,50}... | collective-permute-start | bytes 196616 | tf_op jit(solution)/shard_map/ppermute | solution.py:345
  47.4 6.4 %collective-permute-start.6 = (bf16[4,64,128]{2,1,0:T(8,128)(2,1)S(1)}, bf16[4,64,128]{2,1,0:T(8,128)(2,1)S(1)}, u32[]{:S(2)}, u32[]{:S(2)}) collective-permute-start(bf16[4,64,128]{2,1,0:T(8,128)(2,1)S(1)} %bitcast.47), channel_id=1, source_target_pairs={{0,32},{16,48},{32,0},{48,16},{1,33},{17,49},{33,1},{49,17},{2,34}... | collective-permute-start | bytes 196616 | tf_op jit(solution)/shard_map/ppermute | solution.py:345
  48.0 7.4 %collective-permute-start.5 = (bf16[4,64,128]{2,1,0:T(8,128)(2,1)S(1)}, bf16[4,64,128]{2,1,0:T(8,128)(2,1)S(1)}, u32[]{:S(2)}, u32[]{:S(2)}) collective-permute-start(bf16[4,64,128]{2,1,0:T(8,128)(2,1)S(1)} %bitcast.48), channel_id=1, source_target_pairs={{0,16},{16,32},{32,48},{48,0},{1,17},{17,33},{33,49},{49,1},{2,18}... | collective-permute-start | bytes 196616 | tf_op jit(solution)/shard_map/ppermute | solution.py:345
  56.0 7.1 %collective-permute-start.9 = (bf16[128,32,128]{2,1,0:T(8,128)(2,1)S(1)}, bf16[128,32,128]{2,1,0:T(8,128)(2,1)S(1)}, u32[]{:S(2)}, u32[]{:S(2)}) collective-permute-start(bf16[128,32,128]{2,1,0:T(8,128)(2,1)S(1)} %all-to-all-done), channel_id=1, source_target_pairs={{0,1},{1,0},{2,3},{3,2},{4,5},{5,4},{6,7},{7,6},{8,9},{9,8},{10,11... | collective-permute-start | bytes 3145736 | tf_op jit(solution)/shard_map/ppermute | solution.py:380
  60.6 2.4 %copy-start = (f32[6]{0:T(128)S(1)}, f32[6]{0:T(128)}, u32[]{:S(2)}) copy-start(f32[6]{0:T(128)} %coeff_ref.1) | copy-start | bytes 76
  76.2 6.9 %copy-start.1 = (f32[64,128]{1,0:T(8,128)S(1)}, f32[64,128]{1,0:T(8,128)}, u32[]{:S(2)}) copy-start(f32[64,128]{1,0:T(8,128)} %weights_ref.1) | copy-start | bytes 98308
  76.2 37.3 %all-to-all-start.1 = ((bf16[128,32,128]{2,1,0:T(8,128)(2,1)}), bf16[128,32,128]{2,1,0:T(8,128)(2,1)S(1)}, u32[]{:S(2)}, u32[]{:S(2)}) async-start(bf16[128,32,128]{2,1,0:T(8,128)(2,1)} %bitcast.20), calls=%async_computation.1 | async-start | bytes 2097152 | tf_op jit(solution)/shard_map/all_to_all | solution.py:405
